TPU v7x, 32 devices: a whole 2x2x4 slice. The times are simulated.
32 devices in a mesh: seq: 16 (over z, y, core), head: 2 (over x).
Axes of the slice: x: 2, y: 2, z: 4, core: 2. Of those that a mesh axis runs over, the one named last changes fastest.
Arguments:
- inputs: bfloat16 [2, 4096, 768], P(None, 'seq'), may hold values from -6 to 6
- qkv_weight: bfloat16 [3, 768, 768], P(None, None, 'head'), may hold values from -0.21875 to 0.21875
- qv_bias: float32 [2, 768], P(None, 'head'), may hold values from -3 to 3
- out_weight: bfloat16 [768, 768], P('head'), may hold values from -0.875 to 0.875
- out_bias: float32 [768], replicated, may hold values from -3 to 3
- ln1_gain: float32 [768], replicated, may hold values from 0.25 to 1.75
- ln1_bias: float32 [768], replicated, may hold values from -2 to 2
- ffn_in: bfloat16 [768, 3072], P(None, 'head'), may hold values from -0.21875 to 0.21875
- ffn_in_bias: float32 [3072], P('head'), may hold values from -3 to 3
- ffn_out: bfloat16 [3072, 768], P('head'), may hold values from -0.15625 to 0.15625
- ffn_out_bias: float32 [768], replicated, may hold values from -3 to 3
- ln2_gain: float32 [768], replicated, may hold values from 0.25 to 1.75
- ln2_bias: float32 [768], replicated, may hold values from -2 to 2
- short_lengths: int32 [8], replicated, may hold values from 256 to 512, as said below
- long_lengths: int32 [2], replicated, may hold values from 1024 to 2048, as said below
- short_random: int32 [64, 3], P('seq'), may hold values from 2 to 7, as said below
- long_random: int32 [64, 3], P('seq'), may hold values from 2 to 31, as said below
- cotangent: bfloat16 [2, 4096, 768], P(None, 'seq'), may hold values from -6 to 6
Outputs:
- output: bfloat16 [2, 4096, 768], P(None, 'seq')
- input_grad: bfloat16 [2, 4096, 768], P(None, 'seq')
- qkv_weight_grad: float32 [3, 768, 768], P(None, None, 'head')
- qv_bias_grad: float32 [2, 768], P(None, 'head')
- out_weight_grad: float32 [768, 768], P('head')
- out_bias_grad: float32 [768], replicated
- ln1_gain_grad: float32 [768], replicated
- ln1_bias_grad: float32 [768], replicated
- ffn_in_grad: float32 [768, 3072], P(None, 'head')
- ffn_in_bias_grad: float32 [3072], P('head')
- ffn_out_grad: float32 [3072, 768], P('head')
- ffn_out_bias_grad: float32 [768], replicated
- ln2_gain_grad: float32 [768], replicated
- ln2_bias_grad: float32 [768], replicated
Inputs may be any that keep to these rules, and one draw needn't show every extreme that they name: `short_lengths`: each sequence has between half its padded length 512 and all of it valid; at least one has exactly 512. `long_lengths`: each sequence has between half its padded length 2048 and all of it valid; at least one has exactly 2048. `short_random`: each row holds 3 different block numbers of its own sequence, none below 2 and none within one block of the row's own block. `long_random`: each row holds 3 different block numbers of its own sequence, none below 2 and none within one block of the row's own block.
All inputs are finite; a program needn't handle non-finite values.
Results may differ from a plain program's by a relative error of at most 0.02.
Values may be sent and summed in bfloat16 or wider, within the bound.
A program may use at most 192 MiB of HBM per device.

v0:
```python
import jax
import jax.numpy as jnp
import numpy as np
from jax import lax
from jax.sharding import PartitionSpec as P

HDIM = 64
BLK = 64
GLOB = 2
SBITS = 1
LBITS = 3


EPSILON = 1e-06
NEGATIVE = -1000000000.0


def partner_2(array, axis, distance):
    return lax.ppermute(array, axis, [(i, i ^ 1 << distance) for i in range(lax.axis_size(axis))])


def layer_norm(token_rows, gain, shift):
    centre = jnp.mean(token_rows, axis=-1, keepdims=True)
    centred = token_rows - centre
    spread = jnp.mean(centred * centred, axis=-1, keepdims=True)
    return centred * lax.rsqrt(spread + EPSILON) * gain + shift


def gelu_tanh(entries):
    return jax.nn.gelu(entries, approximate=True)


def group_rows(stacked, level_count):
    position = lax.axis_index("seq")
    for bit_level in range(level_count):
        partner = partner_2(stacked, "seq", bit_level)
        in_upper = position >> bit_level & 1 == 1
        stacked = jnp.where(
            in_upper, jnp.concatenate([partner, stacked], 1), jnp.concatenate([stacked, partner], 1)
        )
    return stacked


def group_sums(whole_grad, level_count):
    position = lax.axis_index("seq")
    for bit_level in reversed(range(level_count)):
        half_rows = whole_grad.shape[1] // 2
        in_upper = position >> bit_level & 1 == 1
        kept_half = jnp.where(in_upper, whole_grad[:, half_rows:], whole_grad[:, :half_rows])
        sent_half = jnp.where(in_upper, whole_grad[:, :half_rows], whole_grad[:, half_rows:])
        whole_grad = kept_half + partner_2(sent_half.astype(jnp.bfloat16), "seq", bit_level).astype(
            sent_half.dtype
        )
    return whole_grad


def masked_scores(queries, key_rows, key_live):
    inv_root = queries.shape[-1] ** (-0.5)
    scores = (
        jnp.einsum("qbhd,qkhd->qhbk", queries, key_rows, preferred_element_type=jnp.float32)
        * inv_root
    )
    return jnp.where(key_live[:, None, None, :], scores, NEGATIVE)


def attend(queries, key_rows, values, key_live):
    scores = masked_scores(queries, key_rows, key_live)
    row_max = jnp.max(scores, axis=-1, keepdims=True)
    weights = jnp.exp(scores - row_max)
    row_total = jnp.sum(weights, axis=-1, keepdims=True)
    probs_low = (weights / row_total).astype(jnp.bfloat16)
    mixed_out = jnp.einsum("qhbk,qkhd->qbhd", probs_low, values, preferred_element_type=jnp.float32)
    return (mixed_out, row_max + jnp.log(row_total))


def attend_back(queries, key_rows, values, key_live, log_total, grad_mixed):
    inv_root = queries.shape[-1] ** (-0.5)
    scores = masked_scores(queries, key_rows, key_live)
    probs = jnp.where(key_live[:, None, None, :], jnp.exp(scores - log_total), 0.0)
    grad_probs = jnp.einsum(
        "qbhd,qkhd->qhbk", grad_mixed, values, preferred_element_type=jnp.float32
    )
    grad_scores = probs * (grad_probs - jnp.sum(probs * grad_probs, axis=-1, keepdims=True))
    scores_low = grad_scores.astype(jnp.bfloat16)
    grad_query = (
        jnp.einsum("qhbk,qkhd->qbhd", scores_low, key_rows, preferred_element_type=jnp.float32)
        * inv_root
    )
    grad_key = (
        jnp.einsum("qhbk,qbhd->qkhd", scores_low, queries, preferred_element_type=jnp.float32)
        * inv_root
    )
    grad_value = jnp.einsum(
        "qhbk,qbhd->qkhd",
        probs.astype(jnp.bfloat16),
        grad_mixed,
        preferred_element_type=jnp.float32,
    )
    return (grad_query, grad_key, grad_value)


def sparse_layout(row_block, table_rows, seq_blocks, seq_length):
    block_count = row_block.shape[0]
    global_ids = jnp.broadcast_to(jnp.arange(GLOB, dtype=jnp.int32)[None, :], (block_count, GLOB))
    nearby = row_block[:, None] + jnp.arange(-1, 2, dtype=jnp.int32)[None, :]
    key_table = jnp.clip(
        jnp.concatenate([global_ids, nearby, table_rows], axis=1), 0, seq_blocks - 1
    )
    slot_live = jnp.concatenate(
        [
            jnp.ones((block_count, GLOB), jnp.bool_),
            (nearby >= GLOB) & (nearby < seq_blocks),
            jnp.ones(table_rows.shape, jnp.bool_),
        ],
        axis=1,
    )
    token_ids = key_table[:, :, None] * BLK + jnp.arange(BLK, dtype=jnp.int32)[None, None, :]
    key_live = (slot_live[:, :, None] & (token_ids < seq_length)).reshape(block_count, -1)
    return (key_table, key_live)


def pack_terms(terms):
    flat = jnp.concatenate([term.reshape(-1) for term in terms])
    return flat


def unpack_terms(flat, layouts):
    pieces = []
    offset = 0
    for dims_here in layouts:
        count_here = int(np.prod(dims_here))
        pieces.append(flat[offset : offset + count_here].reshape(dims_here))
        offset = offset + count_here
    return tuple(pieces)


def body(
    inputs,
    qkv_weight,
    qv_bias,
    out_weight,
    out_bias,
    ln1_gain,
    ln1_bias,
    ffn_in,
    ffn_in_bias,
    ffn_out,
    ffn_out_bias,
    ln2_gain,
    ln2_bias,
    short_lengths,
    long_lengths,
    short_random,
    long_random,
    cotangent,
):
    position = lax.axis_index("seq")
    batches = ((short_lengths, short_random, SBITS), (long_lengths, long_random, LBITS))
    params = (
        qkv_weight,
        qv_bias,
        out_weight,
        out_bias,
        ln1_gain,
        ln1_bias,
        ffn_in,
        ffn_in_bias,
        ffn_out,
        ffn_out_bias,
        ln2_gain,
        ln2_bias,
    )
    layouts = tuple((item.shape for item in params))
    outputs = []
    input_grads = []
    accumulated = None
    shares = None
    for batch_index in range(2):
        lengths, table_rows, level_count = batches[batch_index]
        span_size = 2**level_count
        span_pos = position % span_size
        is_first = span_pos == 0
        seq_length = lengths[position // span_size]
        token_rows = inputs[batch_index]
        rows_wide = token_rows.astype(jnp.float32)
        tok_count = token_rows.shape[0]
        col_width = qkv_weight.shape[2]
        head_count = col_width // HDIM
        block_count = tok_count // BLK
        projected = jnp.einsum(
            "td,cde->cte", token_rows, qkv_weight, preferred_element_type=jnp.float32
        )
        query_low = (projected[0] + qv_bias[0]).astype(jnp.bfloat16)
        kv_pair = jnp.stack([projected[1], projected[2] + qv_bias[1]]).astype(jnp.bfloat16)
        gathered = group_rows(kv_pair, level_count)
        seq_tokens = gathered.shape[1]
        seq_blocks = seq_tokens // BLK
        query_blocks = query_low.reshape(block_count, BLK, head_count, HDIM)
        kv_blocks = gathered.reshape(2, seq_blocks, BLK, head_count, HDIM)
        row_block = span_pos * block_count + jnp.arange(block_count, dtype=jnp.int32)
        key_table, key_live = sparse_layout(row_block, table_rows, seq_blocks, seq_length)
        slot_count = key_table.shape[1]
        sparse_keys = kv_blocks[0][key_table].reshape(
            block_count, slot_count * BLK, head_count, HDIM
        )
        sparse_values = kv_blocks[1][key_table].reshape(
            block_count, slot_count * BLK, head_count, HDIM
        )
        dense_query = query_blocks[:GLOB].reshape(1, GLOB * BLK, head_count, HDIM)
        whole_keys = gathered[0].reshape(1, seq_tokens, head_count, HDIM)
        whole_values = gathered[1].reshape(1, seq_tokens, head_count, HDIM)
        dense_live = (jnp.arange(seq_tokens, dtype=jnp.int32) < seq_length)[None, :]
        sparse_out, sparse_log = attend(query_blocks, sparse_keys, sparse_values, key_live)
        empty_out = jnp.zeros(dense_query.shape, jnp.float32)
        empty_log = jnp.zeros((1, head_count, GLOB * BLK, 1), jnp.float32)
        dense_out, dense_log = lax.cond(
            is_first,
            lambda: attend(dense_query, whole_keys, whole_values, dense_live),
            lambda: (empty_out, empty_log),
        )
        top_rows = jnp.where(
            is_first, dense_out.reshape(GLOB, BLK, head_count, HDIM), sparse_out[:GLOB]
        )
        mixed_low = (
            jnp.concatenate([top_rows, sparse_out[GLOB:]], 0)
            .reshape(tok_count, col_width)
            .astype(jnp.bfloat16)
        )
        attention = lax.psum(
            jnp.dot(mixed_low, out_weight, preferred_element_type=jnp.float32), "head"
        )
        joined = attention + out_bias + rows_wide
        hidden = layer_norm(joined, ln1_gain, ln1_bias)
        hidden_low = hidden.astype(jnp.bfloat16)
        inner = jnp.dot(hidden_low, ffn_in, preferred_element_type=jnp.float32) + ffn_in_bias
        activated = gelu_tanh(inner).astype(jnp.bfloat16)
        feed_out = lax.psum(
            jnp.dot(activated, ffn_out, preferred_element_type=jnp.float32).astype(jnp.bfloat16),
            "head",
        ).astype(jnp.float32)
        second = feed_out + ffn_out_bias + hidden
        outputs.append(layer_norm(second, ln2_gain, ln2_bias).astype(jnp.bfloat16))
        seed_grad = cotangent[batch_index].astype(jnp.float32)
        _, norm_two_back = jax.vjp(layer_norm, second, ln2_gain, ln2_bias)
        grad_second, grad_gain_two, grad_bias_two = norm_two_back(seed_grad)
        grad_feed = grad_second.astype(jnp.bfloat16)
        grad_act = jnp.einsum(
            "td,fd->tf", grad_feed, ffn_out, preferred_element_type=jnp.float32
        ).astype(jnp.bfloat16)
        _, gelu_back = jax.vjp(gelu_tanh, inner)
        grad_inner = gelu_back(grad_act.astype(jnp.float32))[0].astype(jnp.bfloat16)
        hidden_part = jnp.einsum(
            "tf,df->td", grad_inner, ffn_in, preferred_element_type=jnp.float32
        )
        grad_hidden = grad_second + lax.psum(hidden_part.astype(jnp.bfloat16), "head").astype(
            jnp.float32
        )
        _, norm_one_back = jax.vjp(layer_norm, joined, ln1_gain, ln1_bias)
        grad_joined, grad_gain_one, grad_bias_one = norm_one_back(grad_hidden)
        grad_attn = grad_joined.astype(jnp.bfloat16)
        grad_mixed = jnp.einsum(
            "td,cd->tc", grad_attn, out_weight, preferred_element_type=jnp.float32
        ).astype(jnp.bfloat16)
        grad_blocks = grad_mixed.reshape(block_count, BLK, head_count, HDIM)
        zero_top = jnp.zeros_like(grad_blocks[:GLOB])
        sparse_grad = jnp.concatenate(
            [jnp.where(is_first, zero_top, grad_blocks[:GLOB]), grad_blocks[GLOB:]], 0
        )
        dense_grad = grad_blocks[:GLOB].reshape(1, GLOB * BLK, head_count, HDIM)
        sparse_gq, sparse_gk, sparse_gv = attend_back(
            query_blocks, sparse_keys, sparse_values, key_live, sparse_log, sparse_grad
        )
        empty_kv = jnp.zeros(whole_keys.shape, jnp.float32)
        dense_gq, dense_gk, dense_gv = lax.cond(
            is_first,
            lambda: attend_back(
                dense_query, whole_keys, whole_values, dense_live, dense_log, dense_grad
            ),
            lambda: (empty_out, empty_kv, empty_kv),
        )
        grad_query = (
            sparse_gq.at[:GLOB]
            .add(dense_gq.reshape(GLOB, BLK, head_count, HDIM))
            .reshape(tok_count, col_width)
        )
        kv_grad = jnp.zeros((2, seq_blocks, BLK, head_count, HDIM), jnp.float32)
        kv_grad = kv_grad.at[0, key_table].add(
            sparse_gk.reshape(block_count, slot_count, BLK, head_count, HDIM)
        )
        kv_grad = kv_grad.at[1, key_table].add(
            sparse_gv.reshape(block_count, slot_count, BLK, head_count, HDIM)
        )
        kv_grad = kv_grad.reshape(2, seq_tokens, col_width) + jnp.stack(
            [dense_gk, dense_gv]
        ).reshape(2, seq_tokens, col_width)
        kv_local = group_sums(kv_grad, level_count)
        grad_proj = jnp.stack([grad_query, kv_local[0], kv_local[1]]).astype(jnp.bfloat16)
        input_part = jnp.einsum(
            "cte,cde->td", grad_proj, qkv_weight, preferred_element_type=jnp.float32
        )
        grad_rows = grad_joined + lax.psum(input_part.astype(jnp.bfloat16), "head").astype(
            jnp.float32
        )
        input_grads.append(grad_rows.astype(jnp.bfloat16))
        proj_wide = grad_proj.astype(jnp.float32)
        terms = (
            jnp.einsum("td,cte->cde", token_rows, grad_proj, preferred_element_type=jnp.float32),
            jnp.stack([jnp.sum(proj_wide[0], axis=0), jnp.sum(proj_wide[2], axis=0)]),
            jnp.einsum("tc,td->cd", mixed_low, grad_attn, preferred_element_type=jnp.float32),
            jnp.sum(grad_joined, axis=0),
            grad_gain_one,
            grad_bias_one,
            jnp.einsum("td,tf->df", hidden_low, grad_inner, preferred_element_type=jnp.float32),
            jnp.sum(grad_inner.astype(jnp.float32), axis=0),
            jnp.einsum("tf,td->fd", activated, grad_feed, preferred_element_type=jnp.float32),
            jnp.sum(grad_second, axis=0),
            grad_gain_two,
            grad_bias_two,
        )
        accumulated = (
            terms
            if accumulated is None
            else tuple((earlier + fresh for earlier, fresh in zip(accumulated, terms)))
        )
    shares = lax.psum_scatter(pack_terms(accumulated), "seq", scatter_dimension=0, tiled=True)
    flat_total = lax.all_gather(shares.astype(jnp.bfloat16), "seq", axis=0, tiled=True).astype(
        shares.dtype
    )
    totals = unpack_terms(flat_total, layouts)
    return (jnp.stack(outputs), jnp.stack(input_grads)) + tuple(totals)


def solution(mesh):
    return jax.shard_map(
        body,
        mesh=mesh,
        in_specs=(
            P(None, "seq", None),
            P(None, None, "head"),
            P(None, "head"),
            P("head", None),
            P(),
            P(),
            P(),
            P(None, "head"),
            P("head"),
            P("head", None),
            P(),
            P(),
            P(),
            P(),
            P(),
            P("seq", None),
            P("seq", None),
            P(None, "seq", None),
        ),
        out_specs=(
            P(None, "seq", None),
            P(None, "seq", None),
            P(None, None, "head"),
            P(None, "head"),
            P("head", None),
            P(),
            P(),
            P(),
            P(None, "head"),
            P("head"),
            P("head", None),
            P(),
            P(),
            P(),
        ),
        check_vma=False,
    )
```

profile of v0, /device:TPU:0, one launch (start us, length us, event | category | flops | bytes accessed | tf_op | source)
XLA Modules:
  0.0 1252.4 jit_solution(14666307780817759111)
XLA Ops:
  101.0 27.2 %collective-permute-done.3 = bf16[2,1024,384]{1,2,0:T(8,128)(2,1)} collective-permute-done((bf16[2,1024,384]{1,2,0:T(8,128)(2,1)}, bf16[2,1024,384]{1,2,0:T(8,128)(2,1)}, u32[]{:S(2)}, u32[]{:S(2)}) %collective-permute-start.3) | collective-permute-done | bytes 1572896 | tf_op jit(solution)/shard_map/ppermute | solution.py:19
  134.6 5.7 squeeze.53
  160.6 5.7 squeeze.51
  203.1 50.8 %all-reduce.19.cloned.1.call-done = (f32[256,768]{1,0:T(8,128)}, f32[256,768]{1,0:T(8,128)}) async-done(((f32[256,768]{1,0:T(8,128)}, f32[256,768]{1,0:T(8,128)}), (f32[256,768]{1,0:T(8,128)}, f32[256,768]{1,0:T(8,128)})) %all-reduce.19.cloned.1.call-update) | async-done | bytes 1572880 | tf_op jit(solution)/shard_map/psum | solution.py:229
  267.3 29.4 %all-reduce.25.cloned.1.call-done = (bf16[256,768]{1,0:T(8,128)(2,1)}, bf16[256,768]{1,0:T(8,128)(2,1)}) async-done(((bf16[256,768]{1,0:T(8,128)(2,1)}, bf16[256,768]{1,0:T(8,128)(2,1)}), (bf16[256,768]{1,0:T(8,128)(2,1)}, bf16[256,768]{1,0:T(8,128)(2,1)})) %all-reduce.25.cloned.1.call-update) | async-done | bytes 786448 | tf_op jit(solution)/shard_map/psum | solution.py:237
  313.7 5.7 convolution_add_fusion.1
  331.5 6.1 reshape.911
  337.6 22.1 %all-reduce.23.cloned.1.call-done = (bf16[256,768]{1,0:T(8,128)(2,1)}, bf16[256,768]{1,0:T(8,128)(2,1)}) async-done(((bf16[256,768]{1,0:T(8,128)(2,1)}, bf16[256,768]{1,0:T(8,128)(2,1)}), (bf16[256,768]{1,0:T(8,128)(2,1)}, bf16[256,768]{1,0:T(8,128)(2,1)})) %all-reduce.23.cloned.1.call-update) | async-done | bytes 786448 | tf_op jit(solution)/shard_map/psum | solution.py:255
  398.8 6.1 reshape.960
  404.8 6.8 copy.172
  417.2 6.1 reshape.966
  423.3 6.6 copy.175
  429.9 6.1 broadcast_in_dim.217
  436.0 16.1 %scatter_fusion.2 = f32[2,32,64,6,64]{4,2,3,1,0:T(8,128)} fusion(f32[2,32,64,6,64]{4,2,3,1,0:T(8,128)} %broadcast_in_dim.217, s32[32]{0:T(128)S(1)} %reshape.958, f32[32,64,6,64]{3,1,2,0:T(8,128)} %copy.172), kind=kCustom, calls=%fused_computation.6 | custom fusion | flops 786432 | bytes 9437440 | tf_op jit(solution)/shard_map/scatter-add | solution.py:287
  452.1 16.1 %scatter_fusion.3 = f32[2,32,64,6,64]{4,2,3,1,0:T(8,128)} fusion(f32[2,32,64,6,64]{4,2,3,1,0:T(8,128)} %scatter_fusion.2, s32[32]{0:T(128)S(1)} %reshape.964, f32[32,64,6,64]{3,1,2,0:T(8,128)} %copy.175), kind=kCustom, calls=%fused_computation.7 | custom fusion | flops 786432 | bytes 9437440 | tf_op jit(solution)/shard_map/scatter-add | solution.py:290
  468.2 22.9 %copy.203 = f32[2,32,64,6,64]{4,3,2,1,0:T(8,128)} copy(f32[2,32,64,6,64]{4,2,3,1,0:T(8,128)} %scatter_fusion.3) | data formatting | bytes 12582912 | tf_op jit(solution)/shard_map/reshape | solution.py:293
  491.1 13.6 %reshape.998 = f32[2,2048,384]{2,1,0:T(8,128)} reshape(f32[2,32,64,6,64]{4,3,2,1,0:T(8,128)} %copy.203) | data formatting | bytes 12582912 | tf_op jit(solution)/shard_map/reshape | solution.py:293
  504.8 32.3 %conditional.7 = (f32[2,64,6,64]{1,3,2,0:T(8,128)}, f32[1,2048,384]{2,1,0:T(8,128)}, f32[1,2048,384]{2,1,0:T(8,128)}) conditional(s32[]{:T(128)} %convert_element_type.241, () %tuple.70, (pred[2048]{0:T(1024)(128)(4,1)S(1)}, bf16[1,128,6,64]{1,3,2,0:T(8,128)(2,1)S(1)}, bf16[1,2048,6,64]{1,3,2,0:T(8,128)(2,1)}, f32[1,6,128,1]{2,1,3,0:T(8,128)S(1)}, ...), branch_computations={%region_42.43_spmd, %region_43.45_spmd} | conditional | flops 1023196416 | bytes 103820368 | solution.py:274
  555.6 6.8 copy.153
  566.1 6.1 reshape.954
  572.2 6.6 copy.156
  579.2 10.3 scatter_fusion
  589.5 10.5 scatter_fusion.1
  608.8 8.3 conditional.6
  668.3 11.4 dynamic-update-slice.9
  679.7 17.8 %all-reduce.21.cloned.1.call-done = (bf16[256,768]{1,0:T(8,128)(2,1)}, bf16[256,768]{1,0:T(8,128)(2,1)}) async-done(((bf16[256,768]{1,0:T(8,128)(2,1)}, bf16[256,768]{1,0:T(8,128)(2,1)}), (bf16[256,768]{1,0:T(8,128)(2,1)}, bf16[256,768]{1,0:T(8,128)(2,1)})) %all-reduce.21.cloned.1.call-update) | async-done | bytes 786448 | tf_op jit(solution)/shard_map/psum | solution.py:301
  709.2 40.8 %dynamic-update-slice.15 = f32[3545856]{0:T(1024)} dynamic-update-slice(f32[3545856]{0:T(1024)} %add_dynamic-update-slice_fusion, f32[1179648]{0:T(1024)} %reshape.911, s32[]{} %constant.317) | dynamic-update-slice | bytes 9437188
  753.1 297.2 %all-reduce.26 = bf16[3545856]{0:T(1024)(128)(2,1)} all-reduce(f32[3545856]{0:T(1024)} %constant_dynamic-update-slice_fusion.1), channel_id=2, replica_groups=mesh['seq'=16,'head'=2] {'seq'}, use_global_device_ids=true, to_apply=%region_66.67.clone | all-reduce | flops 3545856 | bytes 21275136
  1055.0 7.6 dynamic-update-slice.6
  1065.6 152.3 %all-reduce.17.cloned.1.call-done = bf16[3545856]{0:T(1024)(128)(2,1)} async-done(((bf16[3545856]{0:T(1024)(128)(2,1)}), bf16[3545856]{0:T(1024)(128)(2,1)}) %all-reduce.17.cloned.1.call-update) | async-done | bytes 7091728
  1232.2 5.8 reshape.913
  1238.0 6.1 slice.331
  (558 shorter events, 410.8 us)
Async XLA Ops:
  7.2 251.0 %copy-start = (bf16[1536,768]{1,0:T(8,128)(2,1)S(1)}, bf16[1536,768]{1,0:T(8,128)(2,1)}, u32[]{:S(2)}) copy-start(bf16[1536,768]{1,0:T(8,128)(2,1)} %param.39) | copy-start | bytes 7077892
  7.2 246.7 %all-reduce.19.cloned.1.call-start = ((), (), s32[]{:S(2)}) async-start(), calls=%async_computation.1 | async-start | bytes 3145728 | tf_op jit(solution)/shard_map/psum | solution.py:229
  12.7 24.6 %collective-permute-start.1 = (bf16[2,256,384]{1,2,0:T(8,128)(2,1)}, bf16[2,256,384]{1,2,0:T(8,128)(2,1)}, u32[]{:S(2)}, u32[]{:S(2)}) collective-permute-start(bf16[2,256,384]{1,2,0:T(8,128)(2,1)} %pad_maximum_fusion.6), channel_id=1, source_target_pairs={{0,2},{2,0},{4,6},{6,4},{8,10},{10,8},{12,14},{14,12},{16,18},{18,... | collective-permute-start | bytes 1179656 | tf_op jit(solution)/shard_map/ppermute | solution.py:19
  15.5 32.3 %collective-permute-start = (bf16[2,256,384]{1,2,0:T(8,128)(2,1)}, bf16[2,256,384]{1,2,0:T(8,128)(2,1)}, u32[]{:S(2)}, u32[]{:S(2)}) collective-permute-start(bf16[2,256,384]{1,2,0:T(8,128)(2,1)} %pad_maximum_fusion.4), channel_id=1, source_target_pairs={{0,2},{2,0},{4,6},{6,4},{8,10},{10,8},{12,14},{14,12},{16,18},{18,... | collective-permute-start | bytes 1179656 | tf_op jit(solution)/shard_map/ppermute | solution.py:19
  39.5 50.4 %collective-permute-start.2 = (bf16[2,512,384]{1,2,0:T(8,128)(2,1)}, bf16[2,512,384]{1,2,0:T(8,128)(2,1)}, u32[]{:S(2)}, u32[]{:S(2)}) collective-permute-start(bf16[2,512,384]{1,2,0:T(8,128)(2,1)} %maximum_select_fusion.3), channel_id=1, source_target_pairs={{0,4},{2,6},{4,0},{6,2},{8,12},{10,14},{12,8},{14,10},{16,20},{18,... | collective-permute-start | bytes 2359304 | tf_op jit(solution)/shard_map/ppermute | solution.py:19
  94.6 33.6 %collective-permute-start.3 = (bf16[2,1024,384]{1,2,0:T(8,128)(2,1)}, bf16[2,1024,384]{1,2,0:T(8,128)(2,1)}, u32[]{:S(2)}, u32[]{:S(2)}) collective-permute-start(bf16[2,1024,384]{1,2,0:T(8,128)(2,1)} %maximum_select_fusion.1), channel_id=1, source_target_pairs={{0,8},{2,10},{4,12},{6,14},{8,0},{10,2},{12,4},{14,6},{16,24},{18,... | collective-permute-start | bytes 4718600 | tf_op jit(solution)/shard_map/ppermute | solution.py:19
  197.9 56.0 %copy-start.127 = (f32[768]{0:T(1024)S(1)}, f32[768]{0:T(1024)}, u32[]{:S(2)}) copy-start(f32[768]{0:T(1024)} %param.34) | copy-start | bytes 9220
  201.4 52.4 %copy-start.54 = (bf16[256,384]{0,1:T(8,128)(2,1)}, bf16[256,384]{0,1:T(8,128)(2,1)S(1)}, u32[]{:S(2)}) copy-start(bf16[256,384]{0,1:T(8,128)(2,1)S(1)} %convert_element_type.245) | copy-start | bytes 589828
  202.8 53.7 %copy-start.81 = (f32[768]{0:T(1024)S(1)}, f32[768]{0:T(1024)}, u32[]{:S(2)}) copy-start(f32[768]{0:T(1024)} %param.35) | copy-start | bytes 9220
  202.8 53.6 %copy-start.82 = (f32[768]{0:T(1024)S(1)}, f32[768]{0:T(1024)}, u32[]{:S(2)}) copy-start(f32[768]{0:T(1024)} %param.36) | copy-start | bytes 9220
  202.8 53.6 %copy-start.133 = (f32[1536]{0:T(1024)S(1)}, f32[1536]{0:T(1024)}, u32[]{:S(2)}) copy-start(f32[1536]{0:T(1024)} %param.38) | copy-start | bytes 18436
  202.8 93.9 %all-reduce.25.cloned.1.call-start = ((), (), s32[]{:S(2)}) async-start(), calls=%async_computation.4 | async-start | bytes 1572864 | tf_op jit(solution)/shard_map/psum | solution.py:237
  260.1 36.6 %copy-start.124 = (f32[768]{0:T(1024)S(1)}, f32[768]{0:T(1024)}, u32[]{:S(2)}) copy-start(f32[768]{0:T(1024)} %param.40) | copy-start | bytes 9220
  261.9 97.8 %all-reduce.23.cloned.1.call-start = ((), (), s32[]{:S(2)}) async-start(), calls=%async_computation.3 | async-start | bytes 1572864 | tf_op jit(solution)/shard_map/psum | solution.py:255
  264.8 34.4 %copy-start.99 = (f32[768]{0:T(1024)S(1)}, f32[768]{0:T(1024)}, u32[]{:S(2)}) copy-start(f32[768]{0:T(1024)} %param.41) | copy-start | bytes 9220
  266.7 121.6 %copy-start.83 = (f32[4,6,64]{2,1,0:T(8,128)}, f32[4,6,64]{2,1,0:T(8,128)S(1)}, u32[]{:S(2)}) copy-start(f32[4,6,64]{2,1,0:T(8,128)S(1)} %log_add_fusion.1) | copy-start | bytes 18436
  325.1 372.4 %all-reduce.21.cloned.1.call-start = ((), (), s32[]{:S(2)}) async-start(), calls=%async_computation.2 | async-start | bytes 1572864 | tf_op jit(solution)/shard_map/psum | solution.py:301
  543.9 82.2 %collective-permute-start.5 = (bf16[2,1024,384]{2,1,0:T(8,128)(2,1)}, bf16[2,1024,384]{2,1,0:T(8,128)(2,1)}, u32[]{:S(2)}, u32[]{:S(2)}) collective-permute-start(bf16[2,1024,384]{2,1,0:T(8,128)(2,1)} %select_convert_fusion), channel_id=1, source_target_pairs={{0,8},{2,10},{4,12},{6,14},{8,0},{10,2},{12,4},{14,6},{16,24},{18,... | collective-permute-start | bytes 4718600 | tf_op jit(solution)/shard_map/ppermute | solution.py:19
  620.5 21.1 %collective-permute-start.4 = (bf16[2,256,384]{2,1,0:T(8,128)(2,1)}, bf16[2,256,384]{2,1,0:T(8,128)(2,1)}, u32[]{:S(2)}, u32[]{:S(2)}) collective-permute-start(bf16[2,256,384]{2,1,0:T(8,128)(2,1)} %select_convert_fusion.3), channel_id=1, source_target_pairs={{0,2},{2,0},{4,6},{6,4},{8,10},{10,8},{12,14},{14,12},{16,18},{18,... | collective-permute-start | bytes 1179656 | tf_op jit(solution)/shard_map/ppermute | solution.py:19
  629.1 20.2 %collective-permute-start.6 = (bf16[2,512,384]{2,1,0:T(8,128)(2,1)}, bf16[2,512,384]{2,1,0:T(8,128)(2,1)}, u32[]{:S(2)}, u32[]{:S(2)}) collective-permute-start(bf16[2,512,384]{2,1,0:T(8,128)(2,1)} %select_convert_fusion.1), channel_id=1, source_target_pairs={{0,4},{2,6},{4,0},{6,2},{8,12},{10,14},{12,8},{14,10},{16,20},{18,... | collective-permute-start | bytes 2359304 | tf_op jit(solution)/shard_map/ppermute | solution.py:19
  650.7 2.7 collective-permute-start.7
  664.5 553.4 %all-reduce.17.cloned.1.call-start = ((), (), s32[]{:S(2)}) async-start(), calls=%async_computation | async-start | bytes 14184448
  666.7 34.5 %copy-start.108 = (f32[768]{0:T(1024)S(1)}, f32[768]{0:T(1024)}, u32[]{:S(2)}) copy-start(f32[768]{0:T(1024)} %get-tuple-element.174) | copy-start | bytes 9220
  666.7 34.5 %copy-start.109 = (f32[768]{0:T(1024)S(1)}, f32[768]{0:T(1024)}, u32[]{:S(2)}) copy-start(f32[768]{0:T(1024)} %get-tuple-element.277) | copy-start | bytes 9220
  666.7 35.8 %copy-start.106 = (f32[768]{0:T(1024)S(1)}, f32[768]{0:T(1024)}, u32[]{:S(2)}) copy-start(f32[768]{0:T(1024)} %get-tuple-element.181) | copy-start | bytes 9220
  666.7 35.8 %copy-start.107 = (f32[768]{0:T(1024)S(1)}, f32[768]{0:T(1024)}, u32[]{:S(2)}) copy-start(f32[768]{0:T(1024)} %get-tuple-element.275) | copy-start | bytes 9220
  709.1 40.8 %copy-start.104 = (f32[768]{0:T(1024)S(1)}, f32[768]{0:T(1024)}, u32[]{:S(2)}) copy-start(f32[768]{0:T(1024)} %get-tuple-element.189) | copy-start | bytes 9220
  709.1 40.8 %copy-start.105 = (f32[768]{0:T(1024)S(1)}, f32[768]{0:T(1024)}, u32[]{:S(2)}) copy-start(f32[768]{0:T(1024)} %get-tuple-element.274) | copy-start | bytes 9220
  709.1 42.1 %copy-start.102 = (f32[768]{0:T(1024)S(1)}, f32[768]{0:T(1024)}, u32[]{:S(2)}) copy-start(f32[768]{0:T(1024)} %get-tuple-element.178) | copy-start | bytes 9220
  709.1 42.1 %copy-start.103 = (f32[768]{0:T(1024)S(1)}, f32[768]{0:T(1024)}, u32[]{:S(2)}) copy-start(f32[768]{0:T(1024)} %get-tuple-element.187) | copy-start | bytes 9220
  709.1 43.4 %copy-start.100 = (f32[768]{0:T(1024)S(1)}, f32[768]{0:T(1024)}, u32[]{:S(2)}) copy-start(f32[768]{0:T(1024)} %get-tuple-element.190) | copy-start | bytes 9220
  709.2 43.4 %copy-start.101 = (f32[768]{0:T(1024)S(1)}, f32[768]{0:T(1024)}, u32[]{:S(2)}) copy-start(f32[768]{0:T(1024)} %get-tuple-element.191) | copy-start | bytes 9220
  (117 other events, 631.2 us)
Sparse Core Ops, SparseCore 0:
  202.9 50.9 all-reduce.18
  262.1 34.5 all-reduce.24
  325.2 34.4 all-reduce.22
  664.7 32.8 all-reduce.20
  1062.7 155.1 all-reduce.16
where the time goes:
time: 1270 us; the launch traced here: 1250 us
  local copies, waits for them, and re-layouts  383 us (30%)
  waiting for transfers between devices  304 us (24%)
  blocking collectives  297 us (23%)
  other arithmetic  144 us (11%)
  matrix products  101 us (8%)
  between operations  17.1 us (1%)
    unnamed x1, blocking collectives  297 us
    unnamed x6, waiting for transfers between devices  152 us
    unnamed x273, local copies, waits for them, and re-layouts  86.3 us
    psum x1, waiting for transfers between devices, body(): lax.psum(jnp.dot(mixed_low, out_weight, preferred_element_type=jnp.float3...  50.8 us
    reshape x4, local copies, waits for them, and re-layouts, body(): kv_grad.reshape(2, seq_tokens, col_width)  45.3 us
    ppermute x8, waiting for transfers between devices, partner_2(): lax.ppermute(array, axis, [(i, i ^ 1 << distance) for i in range(lax.axis...  31.4 us
    psum x1, waiting for transfers between devices, body(): lax.psum(jnp.dot(activated, ffn_out, preferred_element_type=jnp.float32)....  29.4 us
    scatter-add x2, other arithmetic, body(): kv_grad.at[1, key_table]  26.5 us
  transfers between devices with their start and end apart: 13, of which 7 were waited for; matrix products, arithmetic and copies ran while one was open for 17% of the time, Pallas kernels for 0%

commit v1 on v0

v1 whole, which is shorter than its diff:
```python
import functools
import math

import jax
import jax.numpy as jnp
from jax import lax
from jax.experimental import pallas as pl
from jax.experimental.pallas import tpu as pltpu
from jax.sharding import PartitionSpec as P

MESH = pl.DeviceIdType.MESH
F32 = jnp.float32
BF16 = jnp.bfloat16
EPSILON = 1e-06
NEGATIVE = -1000000000.0
HDIM = 64
BLK = 64
SHORT, LONG = 0, 1
ROOT = math.sqrt(2.0 / math.pi)
CUBIC = 0.044715
COPIES = 96
VEC_ROWS = 256


def dot(a, b, ca=1, cb=0):
    return lax.dot_general(a, b, (((ca,), (cb,)), ((), ())), preferred_element_type=F32)


def aligned(start, size, step):
    return pl.ds(pl.multiple_of(start, step), size)


def loop(count, step):
    def run(index, carry):
        step(index)
        return carry

    lax.fori_loop(0, count, run, 0)


class Links:
    def __init__(self, send_sem, recv_sem, seq, head):
        self.send_sem, self.recv_sem, self.seq, self.head = send_sem, recv_sem, seq, head
        self.used = 0

    def copy(self, src, dst, seq_delta=0, head_delta=0):
        index = self.used
        self.used += 1
        item = pltpu.make_async_remote_copy(
            src_ref=src,
            dst_ref=dst,
            send_sem=self.send_sem.at[index],
            recv_sem=self.recv_sem.at[index],
            device_id=(self.seq ^ seq_delta, self.head ^ head_delta),
            device_id_type=MESH,
        )
        item.start()
        return item


def add_rows(into, into_start, more, more_start, rows, tile):
    def step(i):
        a = aligned(into_start + i * tile, tile, 16)
        b = aligned(more_start + i * tile, tile, 16)
        into[a, :] = (into[a, :].astype(F32) + more[b, :].astype(F32)).astype(BF16)

    loop(rows // tile, step)


class Reduction:
    def __init__(self, links, part, out, recv_core, recv_next, recv_far, recv_up, upper, local_sem):
        self.links, self.part, self.out = links, part, out
        self.recv_core, self.recv_next, self.recv_far = recv_core, recv_next, recv_far
        self.recv_up, self.upper, self.local_sem = recv_up, upper, local_sem
        rows = part.shape[0]
        self.half, self.quarter, self.share = rows // 2, rows // 4, rows // 16
        self.tile = min(48, self.share)
        seq = links.seq
        core, near, far = seq & 1, (seq >> 1) & 1, (seq >> 2) & 3
        self.core, self.near, self.far = core, near, far
        self.half_at = core * self.half
        self.quarter_at = self.half_at + near * self.quarter
        self.other_quarter_at = self.half_at + (1 - near) * self.quarter
        self.share_at = self.quarter_at + far * self.share
        self.sent = []

    def rows(self, ref, start, count):
        return ref.at[aligned(start, count, 16), :]

    def go(self, src, dst, delta):
        item = self.links.copy(src, dst, delta)
        self.sent.append(item)
        return item

    def start(self):
        self.first = self.go(
            self.rows(self.part, (1 - self.core) * self.half, self.half), self.recv_core, 1
        )

    def over_next(self):
        self.first.wait_recv()
        away = (1 - self.near) * self.quarter
        home = self.near * self.quarter
        add_rows(self.part, self.other_quarter_at, self.recv_core, away, self.quarter, self.tile)
        self.second = self.go(
            self.rows(self.part, self.other_quarter_at, self.quarter), self.recv_next, 2
        )
        add_rows(self.part, self.quarter_at, self.recv_core, home, self.quarter, self.tile)

    def over_far(self):
        self.second.wait_recv()
        self.third = []
        for d in (3, 1, 2):
            there = (self.far ^ d) * self.share
            add_rows(self.part, self.quarter_at + there, self.recv_next, there, self.share, self.tile)
            self.third.append(
                self.go(
                    self.rows(self.part, self.quarter_at + there, self.share),
                    self.recv_far.at[d - 1],
                    4 * d,
                )
            )
        here = self.far * self.share
        add_rows(self.part, self.share_at, self.recv_next, here, self.share, self.tile)

    def total(self):
        for item in self.third:
            item.wait_recv()

        def step(i):
            a = aligned(self.share_at + i * self.tile, self.tile, 16)
            b = aligned(i * self.tile, self.tile, 16)
            total = self.part[a, :].astype(F32)
            for d in range(3):
                total = total + self.recv_far[d, b, :].astype(F32)
            self.part[a, :] = total.astype(BF16)

        loop(self.share // self.tile, step)
        mine = self.rows(self.part, self.share_at, self.share)
        for level, delta in enumerate(self.upper):
            item = self.links.copy(mine, self.recv_up.at[level], delta)
            item.wait()
            add_rows(self.part, self.share_at, self.recv_up.at[level], 0, self.share, self.tile)
        there = self.rows(self.out, self.share_at, self.share)
        self.fourth = [self.go(mine, there, 4 * d) for d in (3, 1, 2)]
        self.kept = pltpu.make_async_copy(mine, there, self.local_sem)
        self.kept.start()

    def back_next(self):
        for item in self.fourth:
            item.wait_recv()
        self.kept.wait()
        block = self.rows(self.out, self.quarter_at, self.quarter)
        self.fifth = self.go(block, block, 2)

    def back_core(self):
        self.fifth.wait_recv()
        block = self.rows(self.out, self.half_at, self.half)
        self.sixth = self.go(block, block, 1)

    def finish(self):
        self.sixth.wait_recv()
        for item in self.sent:
            item.wait_send()


def kernel(
    seq_count,
    x_in,
    cot_in,
    qkvw_in,
    outw_in,
    win_in,
    wout_in,
    qv_bias,
    out_bias,
    gain_one,
    bias_one,
    in_bias,
    back_bias,
    gain_two,
    bias_two,
    short_len,
    long_len,
    short_table,
    long_table,
    out,
    in_grad,
    sum_back,
    sum_in,
    sum_query,
    sum_pair,
    sum_vec,
    x,
    cot,
    qkvw,
    outw,
    win,
    wout,
    kv_short,
    kv_long,
    q_rows,
    q_cols,
    live_short,
    live_long,
    mixed_cols,
    mixed,
    log_total,
    post_out,
    post_in,
    norm_one,
    root_one,
    hidden,
    act,
    slope,
    grad_rows,
    grad_feed,
    grad_inner,
    grad_attn,
    grad_mixed,
    grad_cols,
    dkv_short,
    dkv_long,
    got_short,
    got_core,
    got_far,
    grad_proj,
    part_back,
    part_in,
    part_query,
    part_pair,
    part_vec,
    vec,
    rc_back,
    rc_in,
    rc_query,
    rc_pair,
    rc_vec,
    rn_back,
    rn_in,
    rn_query,
    rn_pair,
    rn_vec,
    rf_back,
    rf_in,
    rf_query,
    rf_pair,
    rf_vec,
    *rest,
):
    upper = [16 << i for i in range(max(0, seq_count.bit_length() - 5))]
    if upper:
        ups = rest[:5]
        rest = rest[5:]
    else:
        ups = (None,) * 5
    send_sem, recv_sem, load_sem, local_sem = rest
    seq, head = lax.axis_index("seq"), lax.axis_index("head")
    links = Links(send_sem, recv_sem, seq, head)
    tok = x.shape[1]
    wide = x.shape[2]
    col = qkvw.shape[2]
    ff = win.shape[1]
    pairs = col // (2 * HDIM)
    blocks = tok // BLK
    short_span = seq_count // short_len.shape[0]
    long_span = seq_count // long_len.shape[0]
    core = seq & 1

    deltas = [1, 2, 4, 6, 8, 12] + upper
    barrier = pltpu.get_barrier_semaphore()
    for delta in deltas:
        pl.semaphore_signal(barrier, inc=1, device_id=(seq ^ delta, head), device_id_type=MESH)
    pl.semaphore_signal(barrier, inc=1, device_id=(seq, head ^ 1), device_id_type=MESH)

    loads = []
    for i, (src, dst) in enumerate(
        ((x_in, x), (qkvw_in, qkvw), (outw_in, outw), (win_in, win), (wout_in, wout), (cot_in, cot))
    ):
        item = pltpu.make_async_copy(src, dst, load_sem.at[i])
        item.start()
        loads.append(item)

    def tokens(mb):
        return pl.ds(mb * tok, tok)

    vec[...] = jnp.zeros_like(vec)
    loads[0].wait()
    loads[1].wait()

    def project(mb, c):
        return dot(x[mb], qkvw[c])

    place = seq & (long_span - 1)
    side = seq & (short_span - 1)
    kv_long[0, place] = project(LONG, 1).astype(BF16)
    kv_long[1, place] = (project(LONG, 2) + qv_bias[1:2, :]).astype(BF16)
    pl.semaphore_wait(barrier, len(deltas) + 1)
    long_direct = {
        d: links.copy(kv_long.at[:, place], kv_long.at[:, place], d) for d in (2, 4, 6)
    }
    long_core = links.copy(kv_long.at[:, place], kv_long.at[:, place], 1)
    kv_short[0, side] = project(SHORT, 1).astype(BF16)
    kv_short[1, side] = (project(SHORT, 2) + qv_bias[1:2, :]).astype(BF16)
    short_core = links.copy(kv_short.at[:, side], kv_short.at[:, side], 1)
    for mb in (SHORT, LONG):
        query = (project(mb, 0) + qv_bias[0:1, :]).astype(BF16).astype(F32) * (HDIM**-0.5)
        q_rows[mb] = query.astype(BF16)
        for g in range(pairs):
            lanes = slice(g * 128, g * 128 + 128)
            q_cols[mb, lanes, :] = query[:, lanes].T.astype(BF16)

    def make_live(live, count, spot, table, length):
        lane_block = lax.broadcasted_iota(jnp.int32, (1, tok), 1) >> 6
        row_block = spot * blocks + lane_block
        picks = []
        for k in range(table.shape[1]):
            pick = jnp.full((1, tok), table[0, k], jnp.int32)
            for b in range(1, blocks):
                pick = jnp.where(lane_block == b, table[b, k], pick)
            picks.append(pick)

        def step(t):
            key = t * tok + lax.broadcasted_iota(jnp.int32, (tok, tok), 0)
            block = key >> 6
            allowed = (block < 2) | (row_block < 2) | (jnp.abs(row_block - block) <= 1)
            for pick in picks:
                allowed = allowed | (block == pick)
            live[t] = jnp.where(allowed & (key < length), 0.0, NEGATIVE)

        loop(count, step)

    make_live(live_short, short_span, side, short_table, short_len[seq // short_span])
    make_live(live_long, long_span, place, long_table, long_len[seq // long_span])

    def spread_cols(pair):
        zero = jnp.zeros((HDIM, tok), BF16)
        return jnp.concatenate(
            [
                jnp.concatenate([pair[:HDIM], zero], 0),
                jnp.concatenate([zero, pair[HDIM:]], 0),
            ],
            1,
        )

    def spread_rows(pair):
        lane = lax.broadcasted_iota(jnp.int32, (tok, 128), 1)
        full = pair.astype(F32)
        return jnp.concatenate(
            [jnp.where(lane < HDIM, full, 0.0), jnp.where(lane < HDIM, 0.0, full)], 0
        ).astype(BF16)

    def attend(mb, kv, live, count):
        def pair_step(g):
            lanes = aligned(g * 128, 128, 128)
            q2 = spread_cols(q_cols[mb, lanes, :])

            def tile_step(t, carry):
                top, total, acc_a, acc_b = carry
                keys = kv[0, t, :, lanes]
                values = kv[1, t, :, lanes]
                mask = live[t]
                scores = dot(keys, q2) + jnp.concatenate([mask, mask], 1)
                new_top = jnp.maximum(top, jnp.max(scores, axis=0, keepdims=True))
                scale = jnp.exp(top - new_top)
                weights = jnp.exp(scores - new_top)
                total = total * scale + jnp.sum(weights, axis=0, keepdims=True)
                low = weights.astype(BF16)
                turned = values.T
                acc_a = acc_a * scale[:, :tok] + dot(turned[:HDIM], low[:, :tok])
                acc_b = acc_b * scale[:, tok:] + dot(turned[HDIM:], low[:, tok:])
                return new_top, total, acc_a, acc_b

            top, total, acc_a, acc_b = lax.fori_loop(
                0,
                count,
                tile_step,
                (
                    jnp.full((1, 2 * tok), -3.0e38, F32),
                    jnp.zeros((1, 2 * tok), F32),
                    jnp.zeros((HDIM, tok), F32),
                    jnp.zeros((HDIM, tok), F32),
                ),
            )
            inverse = 1.0 / total
            pair = jnp.concatenate([acc_a * inverse[:, :tok], acc_b * inverse[:, tok:]], 0)
            mixed_cols[mb, lanes, :] = pair
            mixed[tokens(mb), lanes] = pair.T.astype(BF16)
            log_total[mb * pairs + g] = top + jnp.log(total)

        loop(pairs, pair_step)

    def post(stage, mb):
        buf = stage % 2
        return links.copy(post_out.at[buf, mb], post_in.at[buf, mb], 0, 1)

    def received(stage, mb, rows):
        buf = stage % 2
        return post_out[buf, mb, rows, :].astype(F32) + post_in[buf, mb, rows, :].astype(F32)

    def attention_out(mb):
        post_out[0, mb] = dot(mixed[tokens(mb), :], outw[...]).astype(BF16)
        return post(0, mb)

    short_core.wait()
    attend(SHORT, kv_short, live_short, short_span)
    loads[2].wait()
    posts = {(0, SHORT): attention_out(SHORT)}

    forwards = []
    for d in (2, 4, 6):
        long_direct[d].wait_recv()
        spot = place ^ d
        forwards.append(links.copy(kv_long.at[:, spot], kv_long.at[:, spot], 1))
    long_core.wait()
    for item in forwards:
        item.wait()
    attend(LONG, kv_long, live_long, long_span)
    posts[0, LONG] = attention_out(LONG)
    for d in (2, 4, 6):
        long_direct[d].wait_send()

    def mean(value):
        return jnp.sum(value, axis=-1, keepdims=True) * (1.0 / wide)

    def vec_add(index, value):
        vec[index : index + 1, :wide] += jnp.sum(value, axis=0, keepdims=True)

    OUTB, GAIN1, BIAS1, BACKB, GAIN2, BIAS2 = range(6)

    tile_rows = 64

    def feed_forward(mb):
        posts[0, mb].wait()

        def norm_step(r):
            rows = aligned(r * tile_rows, tile_rows, tile_rows)
            joined = received(0, mb, rows) + out_bias[...] + x[mb, rows, :].astype(F32)
            centred = joined - mean(joined)
            root = lax.rsqrt(mean(centred * centred) + EPSILON)
            normed = centred * root
            norm_one[mb, rows, :] = normed
            root_one[mb, rows, :] = jnp.broadcast_to(root, (tile_rows, 128))
            all_rows = aligned(mb * tok + r * tile_rows, tile_rows, tile_rows)
            hidden[all_rows, :] = (normed * gain_one[...] + bias_one[...]).astype(BF16)

        loop(tok // tile_rows, norm_step)

        def col_step(j):
            lanes = aligned(j * 512, 512, 512)
            u = dot(hidden[tokens(mb), :], win[:, lanes]) + in_bias[:, lanes]
            square = u * u
            t = jnp.tanh(ROOT * u * (1.0 + CUBIC * square))
            half = 0.5 * (1.0 + t)
            act[tokens(mb), lanes] = (u * half).astype(BF16)
            slope[mb, :, lanes] = half + (0.5 * ROOT) * u * (1.0 - t * t) * (
                1.0 + (3.0 * CUBIC) * square
            )

        loop(ff // 512, col_step)
        post_out[1, mb] = dot(act[tokens(mb), :], wout[...]).astype(BF16)
        posts[1, mb] = post(1, mb)

    loads[3].wait()
    loads[4].wait()
    loads[5].wait()
    feed_forward(SHORT)
    feed_forward(LONG)

    def norm_back(grad, normed, root):
        return root * (grad - mean(grad) - normed * mean(grad * normed))

    def feed_back(mb):
        posts[1, mb].wait()

        def norm_step(r):
            rows = aligned(r * tile_rows, tile_rows, tile_rows)
            all_rows = aligned(mb * tok + r * tile_rows, tile_rows, tile_rows)
            hid = norm_one[mb, rows, :] * gain_one[...] + bias_one[...]
            second = received(1, mb, rows) + back_bias[...] + hid
            centred = second - mean(second)
            root = lax.rsqrt(mean(centred * centred) + EPSILON)
            normed = centred * root
            out[mb, rows, :] = (normed * gain_two[...] + bias_two[...]).astype(BF16)
            g = cot[mb, rows, :].astype(F32)
            vec_add(GAIN2, g * normed)
            vec_add(BIAS2, g)
            grad = norm_back(g * gain_two[...], normed, root)
            vec_add(BACKB, grad)
            grad_rows[mb, rows, :] = grad
            grad_feed[all_rows, :] = grad.astype(BF16)

        loop(tok // tile_rows, norm_step)

        def col_step(j):
            lanes = aligned(j * 512, 512, 512)
            grad_act = dot(grad_feed[tokens(mb), :], wout[lanes, :], 1, 1).astype(BF16)
            low = (grad_act.astype(F32) * slope[mb, :, lanes]).astype(BF16)
            grad_inner[tokens(mb), lanes] = low
            vec[6:7, lanes] += jnp.sum(low.astype(F32), axis=0, keepdims=True)

        loop(ff // 512, col_step)
        post_out[0, mb] = dot(grad_inner[tokens(mb), :], win[...], 1, 1).astype(BF16)
        posts[2, mb] = post(2, mb)

    feed_back(SHORT)
    feed_back(LONG)

    def reduction(index, part, total, first, second, third):
        return Reduction(
            links, part, total, first, second, third, ups[index], upper, local_sem.at[index]
        )

    red_back = reduction(0, part_back, sum_back, rc_back, rn_back, rf_back)
    red_in = reduction(1, part_in, sum_in, rc_in, rn_in, rf_in)
    red_query = reduction(2, part_query, sum_query, rc_query, rn_query, rf_query)
    red_pair = reduction(3, part_pair, sum_pair, rc_pair, rn_pair, rf_pair)
    red_vec = reduction(4, part_vec, sum_vec, rc_vec, rn_vec, rf_vec)

    def back_step(j):
        rows = aligned(j * 256, 256, 256)
        part_back[rows, :] = dot(act[:, rows], grad_feed[...], 0, 0).astype(BF16)

    loop(ff // 256, back_step)
    red_back.start()

    def in_step(j):
        rows = aligned(j * 256, 256, 256)
        part_in[rows, :] = dot(hidden[:, rows], grad_inner[...], 0, 0).astype(BF16)

    loop(wide // 256, in_step)
    red_in.start()

    def norm_one_back(mb):
        posts[2, mb].wait()

        def norm_step(r):
            rows = aligned(r * tile_rows, tile_rows, tile_rows)
            all_rows = aligned(mb * tok + r * tile_rows, tile_rows, tile_rows)
            grad = grad_rows[mb, rows, :] + received(2, mb, rows)
            normed = norm_one[mb, rows, :]
            vec_add(GAIN1, grad * normed)
            vec_add(BIAS1, grad)
            joined = norm_back(grad * gain_one[...], normed, root_one[mb, rows, :1])
            vec_add(OUTB, joined)
            grad_rows[mb, rows, :] = joined
            grad_attn[all_rows, :] = joined.astype(BF16)

        loop(tok // tile_rows, norm_step)
        low = dot(grad_attn[tokens(mb), :], outw[...], 1, 1).astype(BF16)
        grad_mixed[...] = low
        for g in range(pairs):
            lanes = slice(g * 128, g * 128 + 128)
            grad_cols[lanes, :] = low[:, lanes].astype(F32).T

    def attend_back(mb, kv, live, count, store):
        def pair_step(g):
            lanes = aligned(g * 128, 128, 128)
            q2 = spread_cols(q_cols[mb, lanes, :])
            cols = grad_cols[lanes, :]
            g2 = spread_cols(cols.astype(BF16))
            q2_rows = spread_rows(q_rows[mb, :, lanes])
            g2_rows = spread_rows(grad_mixed[:, lanes])
            product = cols * mixed_cols[mb, lanes, :]
            delta = jnp.concatenate(
                [
                    jnp.sum(product[:HDIM], axis=0, keepdims=True),
                    jnp.sum(product[HDIM:], axis=0, keepdims=True),
                ],
                1,
            )
            logs = log_total[mb * pairs + g]

            def tile_step(t, carry):
                acc_a, acc_b = carry
                keys = kv[0, t, :, lanes]
                values = kv[1, t, :, lanes]
                mask = live[t]
                scores = dot(keys, q2) + jnp.concatenate([mask, mask], 1)
                probs = jnp.exp(scores - logs)
                grad_probs = dot(values, g2)
                low = (probs * (grad_probs - delta)).astype(BF16)
                store(0, t, lanes, dot(low, q2_rows).astype(BF16))
                store(1, t, lanes, dot(probs.astype(BF16), g2_rows).astype(BF16))
                turned = keys.T
                acc_a = acc_a + dot(turned[:HDIM], low[:, :tok])
                acc_b = acc_b + dot(turned[HDIM:], low[:, tok:])
                return acc_a, acc_b

            acc_a, acc_b = lax.fori_loop(
                0,
                count,
                tile_step,
                (jnp.zeros((HDIM, tok), F32), jnp.zeros((HDIM, tok), F32)),
            )
            pair = jnp.concatenate([acc_a, acc_b], 0) * (HDIM**-0.5)
            grad_proj[tokens(mb), lanes] = pair.T.astype(BF16)

        loop(pairs, pair_step)

    def store_short(which, t, lanes, value):
        dkv_short[which, t, :, lanes] = value

    def store_long(which, t, lanes, value):
        dkv_long[which, t >> 1, t & 1, :, lanes] = value

    norm_one_back(SHORT)
    attend_back(SHORT, kv_short, live_short, short_span, store_short)
    short_grads = links.copy(dkv_short.at[:, 1 - side], got_short, 1)
    red_back.over_next()
    red_in.over_next()
    norm_one_back(LONG)
    attend_back(LONG, kv_long, live_long, long_span, store_long)
    long_grads = links.copy(dkv_long.at[:, :, 1 - core], got_core, 1)

    half_wide = wide // 2

    def out_step(j):
        lanes = aligned(j * half_wide, half_wide, half_wide)
        rows = aligned(j * col, col, col)
        part_query[rows, 0:col] = dot(mixed[...], grad_attn[:, lanes], 0, 0).astype(BF16)

    loop(2, out_step)

    short_grads.wait()
    for which in range(2):
        lanes = slice((1 + which) * col, (2 + which) * col)
        total = dkv_short[which, side].astype(F32) + got_short[which].astype(F32)
        grad_proj[tokens(SHORT), lanes] = total.astype(BF16)

    long_grads.wait()
    mine = (seq >> 1) & 3
    far_grads = []

    def add_far(j):
        for which in range(2):
            dkv_long[which, j, core] = (
                dkv_long[which, j, core].astype(F32) + got_core[which, j].astype(F32)
            ).astype(BF16)

    for d in (3, 1, 2):
        add_far(mine ^ d)
        far_grads.append(
            links.copy(dkv_long.at[:, mine ^ d, core], got_far.at[d - 1], 2 * d)
        )
    add_far(mine)

    def x_grad(part, lanes):
        def step(j):
            rows = aligned(j * 256, 256, 256)
            for mb_part, lanes_here, proj_here in part:
                mb_part[rows, lanes_here] = dot(xs_cols(rows), grad_proj[:, proj_here], 0, 0).astype(
                    BF16
                )

        loop(wide // 256, step)

    def xs_cols(rows):
        return jnp.concatenate([x[0, :, rows], x[1, :, rows]], 0)

    x_grad(((part_query, slice(col, 2 * col), slice(0, col)),), None)
    red_query.start()

    def input_part(mb):
        rows = tokens(mb)
        total = dot(grad_proj[rows, 0:col], qkvw[0], 1, 1)
        total = total + dot(grad_proj[rows, col : 2 * col], qkvw[1], 1, 1)
        total = total + dot(grad_proj[rows, 2 * col : 3 * col], qkvw[2], 1, 1)
        post_out[1, mb] = total.astype(BF16)
        posts[3, mb] = post(3, mb)

    def input_done(mb):
        posts[3, mb].wait()

        def step(r):
            rows = aligned(r * tile_rows, tile_rows, tile_rows)
            in_grad[mb, rows, :] = (grad_rows[mb, rows, :] + received(3, mb, rows)).astype(BF16)

        loop(tok // tile_rows, step)

    input_part(SHORT)
    red_back.over_far()
    red_in.over_far()
    red_query.over_next()

    for item in far_grads:
        item.wait()
    for which in range(2):
        lanes = slice((1 + which) * col, (2 + which) * col)
        total = dkv_long[which, mine, core].astype(F32)
        for d in range(3):
            total = total + got_far[d, which].astype(F32)
        grad_proj[tokens(LONG), lanes] = total.astype(BF16)
    x_grad(
        (
            (part_pair, slice(0, col), slice(col, 2 * col)),
            (part_pair, slice(col, 2 * col), slice(2 * col, 3 * col)),
        ),
        None,
    )
    red_pair.start()

    vec[7:8, 0:col] = jnp.sum(grad_proj[:, 0:col].astype(F32), axis=0, keepdims=True)
    vec[7:8, col : 2 * col] = jnp.sum(
        grad_proj[:, 2 * col : 3 * col].astype(F32), axis=0, keepdims=True
    )
    part_vec[...] = jnp.zeros_like(part_vec)
    row = 0
    lines = []
    for index, width in [(i, wide) for i in range(6)] + [(7, 2 * col), (6, ff)]:
        for k in range(width // 128):
            lines.append(vec[index : index + 1, k * 128 : k * 128 + 128])
    while len(lines) % 16:
        lines.append(jnp.zeros((1, 128), F32))
    part_vec[0 : len(lines), :] = jnp.concatenate(lines, 0).astype(BF16)
    red_vec.start()

    input_part(LONG)
    red_pair.over_next()
    red_vec.over_next()
    red_query.over_far()
    red_back.total()
    red_in.total()
    red_pair.over_far()
    red_vec.over_far()
    input_done(SHORT)
    input_done(LONG)
    red_query.total()
    red_back.back_next()
    red_in.back_next()
    red_pair.total()
    red_vec.total()
    red_query.back_next()
    red_back.back_core()
    red_in.back_core()
    red_pair.back_next()
    red_vec.back_next()
    red_query.back_core()
    red_pair.back_core()
    red_vec.back_core()
    for item in (red_back, red_in, red_query, red_pair, red_vec):
        item.finish()


def body(
    seq_count,
    inputs,
    qkv_weight,
    qv_bias,
    out_weight,
    out_bias,
    ln1_gain,
    ln1_bias,
    ffn_in,
    ffn_in_bias,
    ffn_out,
    ffn_out_bias,
    ln2_gain,
    ln2_bias,
    short_lengths,
    long_lengths,
    short_random,
    long_random,
    cotangent,
):
    tok, wide = inputs.shape[1:]
    col = qkv_weight.shape[2]
    ff = ffn_in.shape[1]
    pairs = col // (2 * HDIM)
    short_span = seq_count // short_lengths.shape[0]
    long_span = seq_count // long_lengths.shape[0]
    upper = max(0, seq_count.bit_length() - 5)

    def row(vector):
        return vector.reshape(1, -1)

    parts = [(ff, wide), (wide, ff), (wide, 2 * col), (wide, 2 * col), (VEC_ROWS, 128)]
    vmem = pltpu.VMEM
    scratch = [
        vmem((2, tok, wide), BF16),
        vmem((2, tok, wide), BF16),
        vmem((3, wide, col), BF16),
        vmem((col, wide), BF16),
        vmem((wide, ff), BF16),
        vmem((ff, wide), BF16),
        vmem((2, short_span, tok, col), BF16),
        vmem((2, long_span, tok, col), BF16),
        vmem((2, tok, col), BF16),
        vmem((2, col, tok), BF16),
        vmem((short_span, tok, tok), F32),
        vmem((long_span, tok, tok), F32),
        vmem((2, col, tok), F32),
        vmem((2 * tok, col), BF16),
        vmem((2 * pairs, 1, 2 * tok), F32),
        vmem((2, 2, tok, wide), BF16),
        vmem((2, 2, tok, wide), BF16),
        vmem((2, tok, wide), F32),
        vmem((2, tok, 128), F32),
        vmem((2 * tok, wide), BF16),
        vmem((2 * tok, ff), BF16),
        vmem((2, tok, ff), F32),
        vmem((2, tok, wide), F32),
        vmem((2 * tok, wide), BF16),
        vmem((2 * tok, ff), BF16),
        vmem((2 * tok, wide), BF16),
        vmem((tok, col), BF16),
        vmem((col, tok), F32),
        vmem((2, short_span, tok, col), BF16),
        vmem((2, long_span // 2, 2, tok, col), BF16),
        vmem((2, tok, col), BF16),
        vmem((2, long_span // 2, tok, col), BF16),
        vmem((long_span // 2 - 1, 2, tok, col), BF16),
        vmem((2 * tok, 3 * col), BF16),
    ]
    scratch += [vmem(shape, BF16) for shape in parts]
    scratch += [vmem((8, ff), F32)]
    scratch += [vmem((r // 2, w), BF16) for r, w in parts]
    scratch += [vmem((r // 4, w), BF16) for r, w in parts]
    scratch += [vmem((3, r // 16, w), BF16) for r, w in parts]
    if upper:
        scratch += [vmem((upper, r // 16, w), BF16) for r, w in parts]
    scratch += [
        pltpu.SemaphoreType.DMA((COPIES,)),
        pltpu.SemaphoreType.DMA((COPIES,)),
        pltpu.SemaphoreType.DMA((8,)),
        pltpu.SemaphoreType.DMA((8,)),
    ]
    any_spec = pl.BlockSpec(memory_space=pl.ANY)
    vmem_spec = pl.BlockSpec(memory_space=pltpu.VMEM)
    smem_spec = pl.BlockSpec(memory_space=pltpu.SMEM)
    out, in_grad, s_back, s_in, s_query, s_pair, s_vec = pl.pallas_call(
        functools.partial(kernel, seq_count),
        out_shape=[
            jax.ShapeDtypeStruct(inputs.shape, BF16),
            jax.ShapeDtypeStruct(inputs.shape, BF16),
        ]
        + [jax.ShapeDtypeStruct(shape, BF16) for shape in parts],
        in_specs=[any_spec] * 6 + [vmem_spec] * 8 + [smem_spec] * 4,
        out_specs=[vmem_spec] * 2 + [any_spec] * 5,
        scratch_shapes=scratch,
        compiler_params=pltpu.CompilerParams(
            collective_id=0, has_side_effects=True, vmem_limit_bytes=63 * 1024 * 1024
        ),
        cost_estimate=pl.CostEstimate(
            flops=12_000_000_000, bytes_accessed=40_000_000, transcendentals=8_000_000
        ),
        name="layer",
    )(
        inputs,
        cotangent,
        qkv_weight,
        out_weight,
        ffn_in,
        ffn_out,
        qv_bias,
        row(out_bias),
        row(ln1_gain),
        row(ln1_bias),
        row(ffn_in_bias),
        row(ffn_out_bias),
        row(ln2_gain),
        row(ln2_bias),
        short_lengths,
        long_lengths,
        short_random,
        long_random,
    )
    qkv_grad = jnp.stack([s_query[:, col:], s_pair[:, :col], s_pair[:, col:]]).astype(F32)
    out_grad = jnp.concatenate([s_query[:col, :col], s_query[col:, :col]], 1).astype(F32)
    flat = s_vec.astype(F32).reshape(-1)
    pieces = [flat[i * wide : (i + 1) * wide] for i in range(6)]
    qv_grad = flat[6 * wide : 6 * wide + 2 * col].reshape(2, col)
    inner_grad = flat[6 * wide + 2 * col : 6 * wide + 2 * col + ff]
    return (
        out,
        in_grad,
        qkv_grad,
        qv_grad,
        out_grad,
        pieces[0],
        pieces[1],
        pieces[2],
        s_in.astype(F32),
        inner_grad,
        s_back.astype(F32),
        pieces[3],
        pieces[4],
        pieces[5],
    )


def solution(mesh):
    return jax.shard_map(
        functools.partial(body, mesh.shape["seq"]),
        mesh=mesh,
        in_specs=(
            P(None, "seq", None),
            P(None, None, "head"),
            P(None, "head"),
            P("head", None),
            P(),
            P(),
            P(),
            P(None, "head"),
            P("head"),
            P("head", None),
            P(),
            P(),
            P(),
            P(),
            P(),
            P("seq", None),
            P("seq", None),
            P(None, "seq", None),
        ),
        out_specs=(
            P(None, "seq", None),
            P(None, "seq", None),
            P(None, None, "head"),
            P(None, "head"),
            P("head", None),
            P(),
            P(),
            P(),
            P(None, "head"),
            P("head"),
            P("head", None),
            P(),
            P(),
            P(),
        ),
        check_vma=False,
    )
```

time: 1270 us -> 240 us (0.19); the launches traced: 1250 us -> 239 us
  local copies, waits for them, and re-layouts: 383 us -> 16.8 us
  waiting for transfers between devices: 304 us -> 0 us
  blocking collectives: 297 us -> 0 us
  Pallas kernels: 0 us -> 212 us
  other arithmetic: 144 us -> 9.38 us
  matrix products: 101 us -> 0 us
  between operations: 17.1 us -> 0.69 us
    unnamed x1 -> x0, blocking collectives: 297 us -> none
    pallas_call x0 -> x1, Pallas kernels: none -> 212 us  [body(): pl.pallas_call(functools.partial(kernel, seq_count), out_shape=[jax.Shape...]
    unnamed x6 -> x0, waiting for transfers between devices: 152 us -> none
    reshape x24 -> x8, local copies, waits for them, and re-layouts: 142 us -> 9.48 us  [the longest x7 8.89 us: row(): return vector.reshape(1, -1)]
    psum x4 -> x0, waiting for transfers between devices: 120 us -> none  [the longest x1 50.8 us: body(): lax.psum(jnp.dot(mixed_low, out_weight, preferred_element_type=jnp.float3...]
    dot_general x50 -> x0, matrix products: 101 us -> none  [the longest x4 13.6 us: attend_back(): jnp.einsum('qbhd,qkhd->qhbk', grad_mixed, values, preferred_element_type=...]
    unnamed x273 -> x12, local copies, waits for them, and re-layouts: 86.3 us -> 2.95 us
    scatter-add x6 -> x0, other arithmetic: 56.3 us -> none  [the longest x2 26.5 us: body(): kv_grad.at[1, key_table]]
  transfers between devices with their start and end apart: 13 -> 0, of which waited for: 7 -> 0; matrix products, arithmetic and copies ran while one was open for 17% -> 0% of each run, Pallas kernels for 0% -> 0%
where the time goes in v1:
time: 240 us; the launch traced here: 239 us
  Pallas kernels  212 us (88%)
  local copies, waits for them, and re-layouts  16.8 us (7%)
  other arithmetic  9.38 us (4%)
    pallas_call x1, Pallas kernels, body(): pl.pallas_call(functools.partial(kernel, seq_count), out_shape=[jax.Shape...  212 us
    reshape x7, local copies, waits for them, and re-layouts, row(): return vector.reshape(1, -1)  8.89 us

profile of v1, /device:TPU:0, one launch (start us, length us, event | category | flops | bytes accessed | tf_op | source)
XLA Modules:
  0.0 239.1 jit_solution(16593292308937242616)
XLA Ops:
  0.6 1.3 reshape.62.out_bias
  1.9 1.3 reshape.63.gain_one
  3.2 1.3 reshape.64.bias_one
  4.4 1.3 reshape.66.back_bias
  5.7 1.3 reshape.67.gain_two
  7.0 1.3 reshape.68.bias_two
  8.2 1.3 reshape.65.in_bias
  9.5 212.3 %layer.1 = (bf16[2,256,768]{2,1,0:T(8,128)(2,1)}, bf16[2,256,768]{2,1,0:T(8,128)(2,1)}, bf16[1536,768]{1,0:T(8,128)(2,1)}, bf16[768,1536]{1,0:T(8,128)(2,1)}, bf...) custom-call(bf16[2,256,768]{2,1,0:T(8,128)(2,1)} %x_in.1, bf16[2,256,768]{2,1,0:T(8,128)(2,1)} %cot_in.1, ...), custom_call_target="tpu_custom_call" | custom-call | flops 12000000000 | bytes 40000000 | tf_op jit(solution)/shard_map/layer/pallas_call | solution.py:831
  221.8 0.0 copy-start.2
  221.8 0.8 slice.81
  222.6 0.6 reshape.69
  223.2 0.8 convert_element_type.16
  224.0 0.6 slice_bitcast_fusion.3
  224.6 0.6 slice_bitcast_fusion.4
  225.3 1.1 fusion
  226.4 0.0 copy-done.2
  226.4 1.2 slice_bitcast_fusion.1
  227.6 1.1 maximum_convert_fusion.1
  228.7 0.0 copy-start.1
  228.7 2.1 maximum_convert_fusion
  230.8 0.6 copy-done.1
  231.4 0.0 copy-start
  231.4 2.8 %convert_element_type.18 = f32[768,1536]{1,0:T(8,128)} convert(bf16[768,1536]{1,0:T(8,128)(2,1)S(1)} %copy-done.1) | non-fusion elementwise | flops 1179648 | bytes 7077888 | tf_op jit(solution)/shard_map/convert_element_type | solution.py:883
  234.3 0.0 copy-done
  234.3 0.0 copy-start.4
  234.3 2.5 %convert_element_type.19 = f32[1536,768]{1,0:T(8,128)} convert(bf16[1536,768]{1,0:T(8,128)(2,1)S(1)} %copy-done) | non-fusion elementwise | flops 1179648 | bytes 7077888 | tf_op jit(solution)/shard_map/convert_element_type | solution.py:885
  236.8 0.0 copy-done.4
  236.8 0.0 copy-start.3
  236.8 0.9 copy.34
  237.7 0.5 copy-done.3
  238.2 0.9 copy.35
Async XLA Ops:
  221.8 4.6 %copy-start.2 = (bf16[768,768]{1,0:T(8,128)(2,1)S(1)}, bf16[768,768]{1,0:T(8,128)(2,1)}, u32[]{:S(2)}) copy-start(bf16[768,768]{1,0:T(8,128)(2,1)} %get-tuple-element.24) | copy-start | bytes 3538948
  228.7 2.7 %copy-start.1 = (bf16[768,1536]{1,0:T(8,128)(2,1)S(1)}, bf16[768,1536]{1,0:T(8,128)(2,1)}, u32[]{:S(2)}) copy-start(bf16[768,1536]{1,0:T(8,128)(2,1)} %get-tuple-element.26) | copy-start | bytes 7077892
  231.4 2.8 %copy-start = (bf16[1536,768]{1,0:T(8,128)(2,1)S(1)}, bf16[1536,768]{1,0:T(8,128)(2,1)}, u32[]{:S(2)}) copy-start(bf16[1536,768]{1,0:T(8,128)(2,1)} %get-tuple-element.27) | copy-start | bytes 7077892
  234.3 2.5 %copy-start.4 = (bf16[2,256,768]{2,1,0:T(8,128)(2,1)S(1)}, bf16[2,256,768]{2,1,0:T(8,128)(2,1)}, u32[]{:S(2)}) copy-start(bf16[2,256,768]{2,1,0:T(8,128)(2,1)} %get-tuple-element.53) | copy-start | bytes 2359300
  236.8 1.4 copy-start.3

commit v2 on v1

v2 whole, which is shorter than its diff:
```python
import functools
import math

import jax
import jax.numpy as jnp
from jax import lax
from jax.experimental import pallas as pl
from jax.experimental.pallas import tpu as pltpu
from jax.sharding import PartitionSpec as P

MESH = pl.DeviceIdType.MESH
F32 = jnp.float32
BF16 = jnp.bfloat16
EPSILON = 1e-06
NEGATIVE = -1000000000.0
HDIM = 64
BLK = 64
SHORT, LONG = 0, 1
ROOT = math.sqrt(2.0 / math.pi)
CUBIC = 0.044715
COPIES = 96
VEC_ROWS = 256


def dot(a, b, ca=1, cb=0):
    return lax.dot_general(a, b, (((ca,), (cb,)), ((), ())), preferred_element_type=F32)


def aligned(start, size, step):
    return pl.ds(pl.multiple_of(start, step), size)


def loop(count, step):
    def run(index, carry):
        step(index)
        return carry

    lax.fori_loop(0, count, run, 0)


class Links:
    def __init__(self, send_sem, recv_sem, seq, head):
        self.send_sem, self.recv_sem, self.seq, self.head = send_sem, recv_sem, seq, head
        self.used = 0

    def copy(self, src, dst, seq_delta=0, head_delta=0):
        index = self.used
        self.used += 1
        item = pltpu.make_async_remote_copy(
            src_ref=src,
            dst_ref=dst,
            send_sem=self.send_sem.at[index],
            recv_sem=self.recv_sem.at[index],
            device_id=(self.seq ^ seq_delta, self.head ^ head_delta),
            device_id_type=MESH,
        )
        item.start()
        return item


def add_rows(into, into_start, more, more_start, rows, tile):
    def step(i):
        a = aligned(into_start + i * tile, tile, 16)
        b = aligned(more_start + i * tile, tile, 16)
        into[a, :] = (into[a, :].astype(F32) + more[b, :].astype(F32)).astype(BF16)

    loop(rows // tile, step)


class Reduction:
    def __init__(self, links, part, out, got, deltas, up, upper, local_sem):
        self.links, self.part, self.out, self.got = links, part, out, got
        self.up, self.upper, self.local_sem = up, upper, local_sem
        self.deltas = deltas
        size = part.shape[0]
        self.tile = min(48, size // 16)
        start = 0
        self.levels = []
        got_at = 0
        for delta in deltas:
            size = size // 2
            upper_half = (links.seq >> (delta.bit_length() - 1)) & 1
            kept, away = start + upper_half * size, start + (1 - upper_half) * size
            self.levels.append((delta, size, start, kept, away, got_at))
            start = kept
            got_at += size
        self.share, self.share_at = size, start
        self.sent = []
        self.last = None

    def rows(self, ref, start, count):
        return ref.at[aligned(start, count, 16), :]

    def go(self, src, dst, delta):
        self.last = self.links.copy(src, dst, delta)
        self.sent.append(self.last)

    def add(self, start, got_start, rows):
        add_rows(self.part, start, self.got, got_start, rows, self.tile)

    def step(self, index):
        delta, size, start, kept, away, got_at = self.levels[index]
        if index:
            self.last.wait_recv()
            got_start = self.levels[index - 1][5]
            self.add(away, got_start + (away - start), size)
        self.go(self.rows(self.part, away, size), self.rows(self.got, got_at, size), delta)
        if index:
            self.add(kept, got_start + (kept - start), size)

    def total(self):
        self.last.wait_recv()
        self.add(self.share_at, self.levels[-1][5], self.share)
        mine = self.rows(self.part, self.share_at, self.share)
        for level, delta in enumerate(self.upper):
            item = self.links.copy(mine, self.up.at[level], delta)
            item.wait()
            add_rows(self.part, self.share_at, self.up.at[level], 0, self.share, self.tile)
        there = self.rows(self.out, self.share_at, self.share)
        self.go(mine, there, self.deltas[-1])
        self.kept = pltpu.make_async_copy(mine, there, self.local_sem)
        self.kept.start()

    def back(self, index):
        self.last.wait_recv()
        if index == len(self.levels) - 2:
            self.kept.wait()
        delta, size, start, kept, away, got_at = self.levels[index]
        block = self.rows(self.out, kept, size)
        self.go(block, block, delta)

    def finish(self):
        self.last.wait_recv()
        for item in self.sent:
            item.wait_send()


def kernel(
    seq_count,
    x_in,
    cot_in,
    qkvw_in,
    outw_in,
    win_in,
    wout_in,
    qv_bias,
    out_bias_in,
    gain_one_in,
    bias_one_in,
    back_bias_in,
    gain_two_in,
    bias_two_in,
    in_bias_in,
    short_len,
    long_len,
    short_table,
    long_table,
    out,
    in_grad,
    sum_back,
    sum_in,
    sum_query,
    sum_pair,
    sum_vec,
    x,
    cot,
    qkvw,
    outw,
    win,
    wout,
    params,
    kv_short,
    kv_long,
    q_cols,
    q_rows,
    live_short,
    live_long,
    mixed_cols,
    mixed,
    tops,
    totals,
    post_out,
    post_in,
    norm_one,
    root_one,
    hidden,
    act,
    slope,
    grad_rows,
    grad_feed,
    grad_inner,
    grad_attn,
    g_cols,
    g_rows,
    deltas,
    query_cols,
    dkv_short,
    dkv_long,
    got_short,
    got_core,
    got_far,
    grad_proj,
    part_back,
    part_in,
    part_query,
    part_pair,
    part_vec,
    vec,
    got_back,
    got_in,
    got_query,
    got_pair,
    got_vec,
    *rest,
):
    upper = [16 << i for i in range(max(0, seq_count.bit_length() - 5))]
    if upper:
        ups = rest[:5]
        rest = rest[5:]
    else:
        ups = (None,) * 5
    send_sem, recv_sem, load_sem, local_sem = rest
    seq, head = lax.axis_index("seq"), lax.axis_index("head")
    links = Links(send_sem, recv_sem, seq, head)
    tok = x.shape[1]
    wide = x.shape[2]
    col = qkvw.shape[2]
    ff = win.shape[1]
    pairs = col // (2 * HDIM)
    blocks = tok // BLK
    short_span = seq_count // short_len.shape[0]
    long_span = seq_count // long_len.shape[0]
    core = seq & 1

    peers = [1, 2, 4, 8] + upper
    barrier = pltpu.get_barrier_semaphore()
    for delta in peers:
        pl.semaphore_signal(barrier, inc=1, device_id=(seq ^ delta, head), device_id_type=MESH)
    pl.semaphore_signal(barrier, inc=1, device_id=(seq, head ^ 1), device_id_type=MESH)

    loads = []
    for i, (src, dst) in enumerate(
        ((x_in, x), (qkvw_in, qkvw), (outw_in, outw), (win_in, win), (wout_in, wout), (cot_in, cot))
    ):
        item = pltpu.make_async_copy(src, dst, load_sem.at[i])
        item.start()
        loads.append(item)

    vectors = (out_bias_in, gain_one_in, bias_one_in, back_bias_in, gain_two_in, bias_two_in)
    for i, vector in enumerate(vectors):
        params[i : i + 1, :wide] = vector[...].reshape(1, wide)
    params[6:7, :] = in_bias_in[...].reshape(1, ff)

    def param(index):
        return params[index : index + 1, :wide]

    OUTB, GAIN1, BIAS1, BACKB, GAIN2, BIAS2 = range(6)

    def tokens(mb):
        return pl.ds(mb * tok, tok)

    vec[...] = jnp.zeros_like(vec)
    loads[0].wait()
    loads[1].wait()

    def project(mb, c):
        return dot(x[mb], qkvw[c])

    place = seq & (long_span - 1)
    side = seq & (short_span - 1)
    kv_long[0, place] = project(LONG, 1).astype(BF16)
    kv_long[1, place] = (project(LONG, 2) + qv_bias[1:2, :]).astype(BF16)
    pl.semaphore_wait(barrier, len(peers) + 1)

    def block(which, spot):
        return kv_long.at[which, spot]

    key_next = links.copy(block(0, place), block(0, place), 2)
    value_far = links.copy(block(1, place), block(1, place), 4)
    value_next = links.copy(block(1, place), block(1, place), 2)
    key_far = links.copy(block(0, place), block(0, place), 4)
    long_core = links.copy(kv_long.at[:, place], kv_long.at[:, place], 1)
    kv_short[0, side] = project(SHORT, 1).astype(BF16)
    kv_short[1, side] = (project(SHORT, 2) + qv_bias[1:2, :]).astype(BF16)
    short_core = links.copy(kv_short.at[:, side], kv_short.at[:, side], 1)

    def spread_cols(pair):
        zero = jnp.zeros((HDIM, tok), BF16)
        return jnp.concatenate(
            [
                jnp.concatenate([pair[:HDIM], zero], 0),
                jnp.concatenate([zero, pair[HDIM:]], 0),
            ],
            1,
        )

    def spread_rows(pair):
        lane = lax.broadcasted_iota(jnp.int32, (tok, 128), 1)
        return jnp.concatenate(
            [jnp.where(lane < HDIM, pair, 0.0), jnp.where(lane < HDIM, 0.0, pair)], 0
        ).astype(BF16)

    for mb in (SHORT, LONG):
        query = (project(mb, 0) + qv_bias[0:1, :]).astype(BF16).astype(F32) * (HDIM**-0.5)
        for g in range(pairs):
            pair = query[:, g * 128 : g * 128 + 128]
            q_rows[mb, g] = spread_rows(pair)
            q_cols[mb, g] = spread_cols(pair.T.astype(BF16))

    def make_live(live, count, spot, table, length):
        lane_block = lax.broadcasted_iota(jnp.int32, (1, tok), 1) >> 6
        row_block = spot * blocks + lane_block
        picks = []
        for k in range(table.shape[1]):
            pick = jnp.full((1, tok), table[0, k], jnp.int32)
            for b in range(1, blocks):
                pick = jnp.where(lane_block == b, table[b, k], pick)
            picks.append(pick)

        def step(t):
            key = t * tok + lax.broadcasted_iota(jnp.int32, (tok, tok), 0)
            key_block = key >> 6
            allowed = (key_block < 2) | (row_block < 2) | (jnp.abs(row_block - key_block) <= 1)
            for pick in picks:
                allowed = allowed | (key_block == pick)
            live[t] = jnp.where(allowed & (key < length), 0.0, NEGATIVE)

        loop(count, step)

    make_live(live_short, short_span, side, short_table, short_len[seq // short_span])
    make_live(live_long, long_span, place, long_table, long_len[seq // long_span])

    def attend(mb, kv, live, spots, first=False):
        def pair_step(g):
            lanes = aligned(g * 128, 128, 128)
            q2 = q_cols[mb, g]
            index = mb * pairs + g
            scores = []
            for t in spots:
                mask = live[t]
                scores.append(dot(kv[0, t, :, lanes], q2) + jnp.concatenate([mask, mask], 1))
            top = functools.reduce(jnp.maximum, [jnp.max(s, axis=0, keepdims=True) for s in scores])
            if not first:
                old = tops[index]
                top = jnp.maximum(old, top)
            tops[index] = top
            total = 0.0
            acc_a = 0.0
            acc_b = 0.0
            for t, s in zip(spots, scores):
                weights = jnp.exp(s - top)
                total = total + jnp.sum(weights, axis=0, keepdims=True)
                low = weights.astype(BF16)
                turned = kv[1, t, :, lanes].T
                acc_a = acc_a + dot(turned[:HDIM], low[:, :tok])
                acc_b = acc_b + dot(turned[HDIM:], low[:, tok:])
            rows_a = aligned(g * 128, HDIM, HDIM)
            rows_b = aligned(g * 128 + HDIM, HDIM, HDIM)
            if not first:
                scale = jnp.exp(old - top)
                total = total + totals[index] * scale
                acc_a = acc_a + mixed_cols[mb, rows_a, :] * scale[:, :tok]
                acc_b = acc_b + mixed_cols[mb, rows_b, :] * scale[:, tok:]
            totals[index] = total
            mixed_cols[mb, rows_a, :] = acc_a
            mixed_cols[mb, rows_b, :] = acc_b

        loop(pairs, pair_step)

    def post(stage, mb):
        buf = stage % 2
        return links.copy(post_out.at[buf, mb], post_in.at[buf, mb], 0, 1)

    def received(stage, mb, rows):
        buf = stage % 2
        return post_out[buf, mb, rows, :].astype(F32) + post_in[buf, mb, rows, :].astype(F32)

    posts = {}

    def attention_out(mb):
        for g in range(pairs):
            index = mb * pairs + g
            lanes = slice(g * 128, g * 128 + 128)
            total = totals[index]
            inverse = 1.0 / total
            pair = jnp.concatenate(
                [
                    mixed_cols[mb, g * 128 : g * 128 + HDIM, :] * inverse[:, :tok],
                    mixed_cols[mb, g * 128 + HDIM : g * 128 + 128, :] * inverse[:, tok:],
                ],
                0,
            )
            mixed_cols[mb, lanes, :] = pair
            mixed[tokens(mb), lanes] = pair.T.astype(BF16)
            tops[index] = tops[index] + jnp.log(total)
        post_out[0, mb] = dot(mixed[tokens(mb), :], outw[...]).astype(BF16)
        posts[0, mb] = post(0, mb)

    short_core.wait()
    attend(SHORT, kv_short, live_short, tuple(range(short_span)), True)
    loads[2].wait()
    attention_out(SHORT)

    key_next.wait_recv()
    key_corner = links.copy(block(0, place ^ 2), block(0, place ^ 2), 4)
    value_far.wait_recv()
    value_corner = links.copy(block(1, place ^ 4), block(1, place ^ 4), 2)
    long_core.wait()
    attend(LONG, kv_long, live_long, (place, place ^ 1), True)
    value_next.wait_recv()
    pass_next = links.copy(kv_long.at[:, place ^ 2], kv_long.at[:, place ^ 2], 1)
    key_far.wait_recv()
    pass_far = links.copy(kv_long.at[:, place ^ 4], kv_long.at[:, place ^ 4], 1)
    attend(LONG, kv_long, live_long, (place ^ 2, place ^ 4))
    pass_next.wait_recv()
    pass_far.wait_recv()
    attend(LONG, kv_long, live_long, (place ^ 3, place ^ 5))
    key_corner.wait_recv()
    value_corner.wait_recv()
    pass_corner = links.copy(kv_long.at[:, place ^ 6], kv_long.at[:, place ^ 6], 1)
    attend(LONG, kv_long, live_long, (place ^ 6,))
    pass_corner.wait_recv()
    attend(LONG, kv_long, live_long, (place ^ 7,))
    attention_out(LONG)
    for item in (
        key_next, value_far, value_next, key_far, key_corner, value_corner,
        pass_next, pass_far, pass_corner,
    ):
        item.wait_send()

    def mean(value):
        return jnp.sum(value, axis=-1, keepdims=True) * (1.0 / wide)

    def vec_add(index, value):
        vec[index : index + 1, :wide] += jnp.sum(value, axis=0, keepdims=True)

    tile_rows = 64

    def feed_forward(mb):
        posts[0, mb].wait()

        def norm_step(r):
            rows = aligned(r * tile_rows, tile_rows, tile_rows)
            joined = received(0, mb, rows) + param(OUTB) + x[mb, rows, :].astype(F32)
            centred = joined - mean(joined)
            root = lax.rsqrt(mean(centred * centred) + EPSILON)
            normed = centred * root
            norm_one[mb, rows, :] = normed
            root_one[mb, rows, :] = jnp.broadcast_to(root, (tile_rows, 128))
            all_rows = aligned(mb * tok + r * tile_rows, tile_rows, tile_rows)
            hidden[all_rows, :] = (normed * param(GAIN1) + param(BIAS1)).astype(BF16)

        loop(tok // tile_rows, norm_step)

        def col_step(j):
            lanes = aligned(j * 512, 512, 512)
            u = dot(hidden[tokens(mb), :], win[:, lanes]) + params[6:7, lanes]
            square = u * u
            t = jnp.tanh(ROOT * u * (1.0 + CUBIC * square))
            half = 0.5 * (1.0 + t)
            act[tokens(mb), lanes] = (u * half).astype(BF16)
            slope[mb, :, lanes] = half + (0.5 * ROOT) * u * (1.0 - t * t) * (
                1.0 + (3.0 * CUBIC) * square
            )

        loop(ff // 512, col_step)
        post_out[1, mb] = dot(act[tokens(mb), :], wout[...]).astype(BF16)
        posts[1, mb] = post(1, mb)

    loads[3].wait()
    loads[4].wait()
    loads[5].wait()
    feed_forward(SHORT)
    feed_forward(LONG)

    def norm_back(grad, normed, root):
        return root * (grad - mean(grad) - normed * mean(grad * normed))

    def feed_norm(mb):
        posts[1, mb].wait()

        def norm_step(r):
            rows = aligned(r * tile_rows, tile_rows, tile_rows)
            all_rows = aligned(mb * tok + r * tile_rows, tile_rows, tile_rows)
            hid = norm_one[mb, rows, :] * param(GAIN1) + param(BIAS1)
            second = received(1, mb, rows) + param(BACKB) + hid
            centred = second - mean(second)
            root = lax.rsqrt(mean(centred * centred) + EPSILON)
            normed = centred * root
            out[mb, rows, :] = (normed * param(GAIN2) + param(BIAS2)).astype(BF16)
            g = cot[mb, rows, :].astype(F32)
            vec_add(GAIN2, g * normed)
            vec_add(BIAS2, g)
            grad = norm_back(g * param(GAIN2), normed, root)
            vec_add(BACKB, grad)
            grad_rows[mb, rows, :] = grad
            grad_feed[all_rows, :] = grad.astype(BF16)

        loop(tok // tile_rows, norm_step)

    def feed_back(mb):
        def col_step(j):
            lanes = aligned(j * 512, 512, 512)
            grad_act = dot(grad_feed[tokens(mb), :], wout[lanes, :], 1, 1).astype(BF16)
            low = (grad_act.astype(F32) * slope[mb, :, lanes]).astype(BF16)
            grad_inner[tokens(mb), lanes] = low
            vec[6:7, lanes] += jnp.sum(low.astype(F32), axis=0, keepdims=True)

        loop(ff // 512, col_step)
        post_out[0, mb] = dot(grad_inner[tokens(mb), :], win[...], 1, 1).astype(BF16)
        posts[2, mb] = post(2, mb)

    feed_norm(SHORT)
    feed_back(SHORT)

    def reduction(index, part, total, got, order):
        return Reduction(links, part, total, got, order, ups[index], upper, local_sem.at[index])

    near_first, far_first = (1, 2, 4, 8), (1, 4, 8, 2)
    red_back = reduction(0, part_back, sum_back, got_back, near_first)
    red_in = reduction(1, part_in, sum_in, got_in, near_first)
    red_query = reduction(2, part_query, sum_query, got_query, far_first)
    red_pair = reduction(3, part_pair, sum_pair, got_pair, near_first)
    red_vec = reduction(4, part_vec, sum_vec, got_vec, near_first)

    feed_norm(LONG)

    def back_step(j):
        rows = aligned(j * 256, 256, 256)
        part_back[rows, :] = dot(act[:, rows], grad_feed[...], 0, 0).astype(BF16)

    loop(ff // 256, back_step)
    red_back.step(0)
    feed_back(LONG)

    def in_step(j):
        rows = aligned(j * 256, 256, 256)
        part_in[rows, :] = dot(hidden[:, rows], grad_inner[...], 0, 0).astype(BF16)

    red_back.step(1)
    loop(wide // 256, in_step)
    red_in.step(0)

    def norm_one_back(mb):
        posts[2, mb].wait()

        def norm_step(r):
            rows = aligned(r * tile_rows, tile_rows, tile_rows)
            all_rows = aligned(mb * tok + r * tile_rows, tile_rows, tile_rows)
            grad = grad_rows[mb, rows, :] + received(2, mb, rows)
            normed = norm_one[mb, rows, :]
            vec_add(GAIN1, grad * normed)
            vec_add(BIAS1, grad)
            joined = norm_back(grad * param(GAIN1), normed, root_one[mb, rows, :1])
            vec_add(OUTB, joined)
            grad_rows[mb, rows, :] = joined
            grad_attn[all_rows, :] = joined.astype(BF16)

        loop(tok // tile_rows, norm_step)
        low = dot(grad_attn[tokens(mb), :], outw[...], 1, 1).astype(BF16).astype(F32)
        for g in range(pairs):
            pair = low[:, g * 128 : g * 128 + 128]
            turned = pair.T
            g_rows[g] = spread_rows(pair)
            g_cols[g] = spread_cols(turned.astype(BF16))
            product = turned * mixed_cols[mb, g * 128 : g * 128 + 128, :]
            deltas[g] = jnp.concatenate(
                [
                    jnp.sum(product[:HDIM], axis=0, keepdims=True),
                    jnp.sum(product[HDIM:], axis=0, keepdims=True),
                ],
                1,
            )

    def attend_back(mb, kv, live, t, store, first=False):
        def pair_step(g):
            lanes = aligned(g * 128, 128, 128)
            keys = kv[0, t, :, lanes]
            values = kv[1, t, :, lanes]
            mask = live[t]
            scores = dot(keys, q_cols[mb, g]) + jnp.concatenate([mask, mask], 1)
            probs = jnp.exp(scores - tops[mb * pairs + g])
            grad_probs = dot(values, g_cols[g])
            low = (probs * (grad_probs - deltas[g])).astype(BF16)
            store(0, lanes, dot(low, q_rows[mb, g]).astype(BF16))
            store(1, lanes, dot(probs.astype(BF16), g_rows[g]).astype(BF16))
            turned = keys.T
            rows_a = aligned(g * 128, HDIM, HDIM)
            rows_b = aligned(g * 128 + HDIM, HDIM, HDIM)
            acc_a = dot(turned[:HDIM], low[:, :tok])
            acc_b = dot(turned[HDIM:], low[:, tok:])
            if not first:
                acc_a = acc_a + query_cols[rows_a, :]
                acc_b = acc_b + query_cols[rows_b, :]
            query_cols[rows_a, :] = acc_a
            query_cols[rows_b, :] = acc_b

        loop(pairs, pair_step)

    def query_done(mb):
        for g in range(pairs):
            lanes = slice(g * 128, g * 128 + 128)
            grad_proj[tokens(mb), lanes] = (query_cols[lanes, :] * (HDIM**-0.5)).T.astype(BF16)

    def store_short(t):
        def store(which, lanes, value):
            dkv_short[which, t, :, lanes] = value

        return store

    def store_long(j, c):
        def store(which, lanes, value):
            dkv_long[which, j, c, :, lanes] = value

        return store

    norm_one_back(SHORT)
    attend_back(SHORT, kv_short, live_short, 1 - side, store_short(1 - side), True)
    short_grads = links.copy(dkv_short.at[:, 1 - side], got_short, 1)
    attend_back(SHORT, kv_short, live_short, side, store_short(side))
    query_done(SHORT)
    red_in.step(1)
    red_back.step(2)
    norm_one_back(LONG)
    mine = (seq >> 1) & 3

    def add_block(which, j, more):
        dkv_long[which, j, core] = (
            dkv_long[which, j, core].astype(F32) + more[...].astype(F32)
        ).astype(BF16)

    def go_far(which, j, slot, delta):
        return links.copy(dkv_long.at[which, j, core], got_far.at[slot], delta)

    core_grads = []
    key_hop = []
    value_hop = []
    for order, d in enumerate((3, 1, 2, 0)):
        j = mine ^ d
        attend_back(LONG, kv_long, live_long, 2 * j + 1 - core, store_long(j, 1 - core), order == 0)
        item = links.copy(dkv_long.at[:, j, 1 - core], got_core.at[:, j], 1)
        core_grads.append(item)
        attend_back(LONG, kv_long, live_long, 2 * j + core, store_long(j, core))
        item.wait_recv()
        for which in range(2):
            add_block(which, j, got_core.at[which, j])
        if d == 1:
            key_hop = [go_far(0, mine ^ 3, 0, 2), go_far(0, mine ^ 1, 1, 2)]
        if d == 2:
            value_hop = [go_far(1, mine ^ 3, 2, 4), go_far(1, mine ^ 2, 3, 4)]
    query_done(LONG)
    key_hop[0].wait_recv()
    add_block(0, mine ^ 2, got_far.at[0])
    key_hop.append(go_far(0, mine ^ 2, 4, 4))
    value_hop[0].wait_recv()
    add_block(1, mine ^ 1, got_far.at[2])
    value_hop.append(go_far(1, mine ^ 1, 5, 2))

    half_wide = wide // 2

    def out_step(j):
        lanes = aligned(j * half_wide, half_wide, half_wide)
        rows = aligned(j * col, col, col)
        part_query[rows, 0:col] = dot(mixed[...], grad_attn[:, lanes], 0, 0).astype(BF16)

    loop(2, out_step)

    def x_grad(items):
        def step(j):
            rows = aligned(j * 256, 256, 256)
            columns = jnp.concatenate([x[0, :, rows], x[1, :, rows]], 0)
            for part, lanes, source in items:
                part[rows, lanes] = dot(columns, grad_proj[:, source], 0, 0).astype(BF16)

        loop(wide // 256, step)

    x_grad([(part_query, slice(col, 2 * col), slice(0, col))])
    red_query.step(0)

    short_grads.wait()
    for which in range(2):
        lanes = slice((1 + which) * col, (2 + which) * col)
        total = dkv_short[which, side].astype(F32) + got_short[which].astype(F32)
        grad_proj[tokens(SHORT), lanes] = total.astype(BF16)

    def input_part(mb):
        rows = tokens(mb)
        total = dot(grad_proj[rows, 0:col], qkvw[0], 1, 1)
        total = total + dot(grad_proj[rows, col : 2 * col], qkvw[1], 1, 1)
        total = total + dot(grad_proj[rows, 2 * col : 3 * col], qkvw[2], 1, 1)
        post_out[1, mb] = total.astype(BF16)
        posts[3, mb] = post(3, mb)

    def input_done(mb):
        posts[3, mb].wait()

        def step(r):
            rows = aligned(r * tile_rows, tile_rows, tile_rows)
            in_grad[mb, rows, :] = (grad_rows[mb, rows, :] + received(3, mb, rows)).astype(BF16)

        loop(tok // tile_rows, step)

    input_part(SHORT)
    red_in.step(2)
    red_back.step(3)
    red_query.step(1)

    for hop, which in ((key_hop, 0), (value_hop, 1)):
        lanes = slice((1 + which) * col, (2 + which) * col)
        hop[1].wait_recv()
        hop[2].wait_recv()
        total = dkv_long[which, mine, core].astype(F32) + got_far[2 * which + 1].astype(F32)
        total = total + got_far[4 + which].astype(F32)
        grad_proj[tokens(LONG), lanes] = total.astype(BF16)
    x_grad(
        [
            (part_pair, slice(0, col), slice(col, 2 * col)),
            (part_pair, slice(col, 2 * col), slice(2 * col, 3 * col)),
        ]
    )
    red_pair.step(0)

    vec[7:8, 0:col] = jnp.sum(grad_proj[:, 0:col].astype(F32), axis=0, keepdims=True)
    vec[7:8, col : 2 * col] = jnp.sum(
        grad_proj[:, 2 * col : 3 * col].astype(F32), axis=0, keepdims=True
    )
    part_vec[...] = jnp.zeros_like(part_vec)
    lines = []
    for index, width in [(i, wide) for i in range(6)] + [(7, 2 * col), (6, ff)]:
        for k in range(width // 128):
            lines.append(vec[index : index + 1, k * 128 : k * 128 + 128])
    while len(lines) % 16:
        lines.append(jnp.zeros((1, 128), F32))
    part_vec[0 : len(lines), :] = jnp.concatenate(lines, 0).astype(BF16)
    red_vec.step(0)
    input_part(LONG)

    red_back.total()
    red_pair.step(1)
    red_vec.step(1)
    red_in.step(3)
    red_query.step(2)
    red_back.back(2)
    input_done(SHORT)
    red_in.total()
    red_pair.step(2)
    red_vec.step(2)
    red_query.step(3)
    red_back.back(1)
    red_in.back(2)
    red_pair.step(3)
    red_vec.step(3)
    red_query.total()
    red_in.back(1)
    red_pair.total()
    red_vec.total()
    red_query.back(2)
    input_done(LONG)
    red_pair.back(2)
    red_vec.back(2)
    red_back.back(0)
    red_query.back(1)
    red_pair.back(1)
    red_vec.back(1)
    red_in.back(0)
    red_query.back(0)
    red_pair.back(0)
    red_vec.back(0)
    for item in (red_back, red_in, red_query, red_pair, red_vec):
        item.finish()
    for item in core_grads + key_hop + value_hop:
        item.wait_send()


def widen(back, inner, query, out_low, out_high, pair, vec, out_in, grad_in, *outs):
    out, in_grad, g_back, g_inner, g_qkv, g_out, g_qv, g_in_bias, *vectors = outs
    col = query.shape[1]
    wide = vectors[0].shape[0]
    out[...] = out_in[...]
    in_grad[...] = grad_in[...]
    g_back[...] = back[...].astype(F32)
    g_inner[...] = inner[...].astype(F32)
    g_qkv[0] = query[...].astype(F32)
    g_qkv[1] = pair[:, :col].astype(F32)
    g_qkv[2] = pair[:, col:].astype(F32)
    g_out[:, :col] = out_low[...].astype(F32)
    g_out[:, col:] = out_high[...].astype(F32)

    @pl.when(pl.program_id(0) == 0)
    def _():
        full = vec[...].astype(F32)

        def line(row, count):
            return jnp.concatenate([full[r : r + 1, :] for r in range(row, row + count)], 1)

        per = wide // 128
        for i, vector in enumerate(vectors):
            vector[...] = line(i * per, per).reshape(wide)
        row = len(vectors) * per
        g_qv[...] = jnp.concatenate(
            [line(row, col // 128), line(row + col // 128, col // 128)], 0
        )
        g_in_bias[...] = line(row + 2 * col // 128, g_in_bias.shape[0] // 128).reshape(
            g_in_bias.shape[0]
        )


def body(
    seq_count,
    inputs,
    qkv_weight,
    qv_bias,
    out_weight,
    out_bias,
    ln1_gain,
    ln1_bias,
    ffn_in,
    ffn_in_bias,
    ffn_out,
    ffn_out_bias,
    ln2_gain,
    ln2_bias,
    short_lengths,
    long_lengths,
    short_random,
    long_random,
    cotangent,
):
    tok, wide = inputs.shape[1:]
    col = qkv_weight.shape[2]
    ff = ffn_in.shape[1]
    pairs = col // (2 * HDIM)
    short_span = seq_count // short_lengths.shape[0]
    long_span = seq_count // long_lengths.shape[0]
    upper = max(0, seq_count.bit_length() - 5)

    parts = [(ff, wide), (wide, ff), (wide, 2 * col), (wide, 2 * col), (VEC_ROWS, 128)]
    vmem = pltpu.VMEM
    scratch = [
        vmem((2, tok, wide), BF16),
        vmem((2, tok, wide), BF16),
        vmem((3, wide, col), BF16),
        vmem((col, wide), BF16),
        vmem((wide, ff), BF16),
        vmem((ff, wide), BF16),
        vmem((8, ff), F32),
        vmem((2, short_span, tok, col), BF16),
        vmem((2, long_span, tok, col), BF16),
        vmem((2, pairs, 128, 2 * tok), BF16),
        vmem((2, pairs, 2 * tok, 128), BF16),
        vmem((short_span, tok, tok), F32),
        vmem((long_span, tok, tok), F32),
        vmem((2, col, tok), F32),
        vmem((2 * tok, col), BF16),
        vmem((2 * pairs, 1, 2 * tok), F32),
        vmem((2 * pairs, 1, 2 * tok), F32),
        vmem((2, 2, tok, wide), BF16),
        vmem((2, 2, tok, wide), BF16),
        vmem((2, tok, wide), F32),
        vmem((2, tok, 128), F32),
        vmem((2 * tok, wide), BF16),
        vmem((2 * tok, ff), BF16),
        vmem((2, tok, ff), F32),
        vmem((2, tok, wide), F32),
        vmem((2 * tok, wide), BF16),
        vmem((2 * tok, ff), BF16),
        vmem((2 * tok, wide), BF16),
        vmem((pairs, 128, 2 * tok), BF16),
        vmem((pairs, 2 * tok, 128), BF16),
        vmem((pairs, 1, 2 * tok), F32),
        vmem((col, tok), F32),
        vmem((2, short_span, tok, col), BF16),
        vmem((2, long_span // 2, 2, tok, col), BF16),
        vmem((2, tok, col), BF16),
        vmem((2, long_span // 2, tok, col), BF16),
        vmem((6, tok, col), BF16),
        vmem((2 * tok, 3 * col), BF16),
    ]
    scratch += [vmem(shape, BF16) for shape in parts]
    scratch += [vmem((8, ff), F32)]
    scratch += [vmem((r - r // 16, w), BF16) for r, w in parts]
    if upper:
        scratch += [vmem((upper, r // 16, w), BF16) for r, w in parts]
    scratch += [
        pltpu.SemaphoreType.DMA((COPIES,)),
        pltpu.SemaphoreType.DMA((COPIES,)),
        pltpu.SemaphoreType.DMA((8,)),
        pltpu.SemaphoreType.DMA((8,)),
    ]
    any_spec = pl.BlockSpec(memory_space=pl.ANY)
    vmem_spec = pl.BlockSpec(memory_space=pltpu.VMEM)
    smem_spec = pl.BlockSpec(memory_space=pltpu.SMEM)
    out, in_grad, s_back, s_in, s_query, s_pair, s_vec = pl.pallas_call(
        functools.partial(kernel, seq_count),
        out_shape=[
            jax.ShapeDtypeStruct(inputs.shape, BF16),
            jax.ShapeDtypeStruct(inputs.shape, BF16),
        ]
        + [jax.ShapeDtypeStruct(shape, BF16) for shape in parts],
        in_specs=[any_spec] * 6 + [vmem_spec] * 8 + [smem_spec] * 4,
        out_specs=[vmem_spec] * 2 + [any_spec] * 5,
        scratch_shapes=scratch,
        compiler_params=pltpu.CompilerParams(
            collective_id=0, has_side_effects=True, vmem_limit_bytes=63 * 1024 * 1024
        ),
        cost_estimate=pl.CostEstimate(
            flops=12_000_000_000, bytes_accessed=40_000_000, transcendentals=8_000_000
        ),
        name="layer",
    )(
        inputs,
        cotangent,
        qkv_weight,
        out_weight,
        ffn_in,
        ffn_out,
        qv_bias,
        out_bias,
        ln1_gain,
        ln1_bias,
        ffn_out_bias,
        ln2_gain,
        ln2_bias,
        ffn_in_bias,
        short_lengths,
        long_lengths,
        short_random,
        long_random,
    )
    steps = 8
    vector = jax.ShapeDtypeStruct((wide,), F32)
    whole = pl.BlockSpec(memory_space=pltpu.VMEM)
    rows_spec = pl.BlockSpec((2, tok // steps, wide), lambda i: (0, i, 0))
    out, in_grad, g_back, g_inner, g_qkv, g_out, g_qv, g_in_bias, *vectors = pl.pallas_call(
        widen,
        grid=(steps,),
        out_shape=[
            jax.ShapeDtypeStruct(inputs.shape, BF16),
            jax.ShapeDtypeStruct(inputs.shape, BF16),
            jax.ShapeDtypeStruct((ff, wide), F32),
            jax.ShapeDtypeStruct((wide, ff), F32),
            jax.ShapeDtypeStruct((3, wide, col), F32),
            jax.ShapeDtypeStruct((col, wide), F32),
            jax.ShapeDtypeStruct((2, col), F32),
            jax.ShapeDtypeStruct((ff,), F32),
        ]
        + [vector] * 6,
        in_specs=[
            pl.BlockSpec((ff // steps, wide), lambda i: (i, 0)),
            pl.BlockSpec((wide // steps, ff), lambda i: (i, 0)),
            pl.BlockSpec((wide // steps, col), lambda i: (i, 1)),
            pl.BlockSpec((col // steps, col), lambda i: (i, 0)),
            pl.BlockSpec((col // steps, col), lambda i: (i + steps, 0)),
            pl.BlockSpec((wide // steps, 2 * col), lambda i: (i, 0)),
            whole,
            rows_spec,
            rows_spec,
        ],
        out_specs=[
            rows_spec,
            rows_spec,
            pl.BlockSpec((ff // steps, wide), lambda i: (i, 0)),
            pl.BlockSpec((wide // steps, ff), lambda i: (i, 0)),
            pl.BlockSpec((3, wide // steps, col), lambda i: (0, i, 0)),
            pl.BlockSpec((col // steps, wide), lambda i: (i, 0)),
        ]
        + [whole] * 8,
        compiler_params=pltpu.CompilerParams(vmem_limit_bytes=63 * 1024 * 1024),
        name="widen",
    )(s_back, s_in, s_query, s_query, s_query, s_pair, s_vec, out, in_grad)
    return (
        out,
        in_grad,
        g_qkv,
        g_qv,
        g_out,
        vectors[0],
        vectors[1],
        vectors[2],
        g_inner,
        g_in_bias,
        g_back,
        vectors[3],
        vectors[4],
        vectors[5],
    )


def solution(mesh):
    return jax.shard_map(
        functools.partial(body, mesh.shape["seq"]),
        mesh=mesh,
        in_specs=(
            P(None, "seq", None),
            P(None, None, "head"),
            P(None, "head"),
            P("head", None),
            P(),
            P(),
            P(),
            P(None, "head"),
            P("head"),
            P("head", None),
            P(),
            P(),
            P(),
            P(),
            P(),
            P("seq", None),
            P("seq", None),
            P(None, "seq", None),
        ),
        out_specs=(
            P(None, "seq", None),
            P(None, "seq", None),
            P(None, None, "head"),
            P(None, "head"),
            P("head", None),
            P(),
            P(),
            P(),
            P(None, "head"),
            P("head"),
            P("head", None),
            P(),
            P(),
            P(),
        ),
        check_vma=False,
    )
```

time: 240 us -> 185 us (0.77)
  Pallas kernels: 212 us -> 184 us
  local copies, waits for them, and re-layouts: 16.8 us -> 0 us
  other arithmetic: 9.38 us -> 0 us
    pallas_call x1, Pallas kernels: 212 us -> 173 us  [body(): pl.pallas_call(functools.partial(kernel, seq_count), out_shape=[jax.Shape...]
    pallas_call x0 -> x1, Pallas kernels: none -> 10.5 us  [body(): pl.pallas_call(widen, grid=(steps,), out_shape=[jax.ShapeDtypeStruct(inpu...]
    reshape x8 -> x0, local copies, waits for them, and re-layouts: 9.48 us -> none  [the longest x7 8.89 us: row(): return vector.reshape(1, -1)]
    convert_element_type x5 -> x0, other arithmetic: 9.38 us -> none  [the longest x1 2.82 us: body(): s_in.astype(F32)]
    slice x4 -> x0, local copies, waits for them, and re-layouts: 3.1 us -> none  [the longest x1 1.11 us: body(): s_query[:col, :col]]
    unnamed x12 -> x0, local copies, waits for them, and re-layouts: 2.95 us -> none
where the time goes in v2:
time: 185 us
  Pallas kernels  184 us (99%)
    pallas_call x1, Pallas kernels, body(): pl.pallas_call(functools.partial(kernel, seq_count), out_shape=[jax.Shape...  173 us
    pallas_call x1, Pallas kernels, body(): pl.pallas_call(widen, grid=(steps,), out_shape=[jax.ShapeDtypeStruct(inpu...  10.5 us

profile of v2, /device:TPU:0, one launch (start us, length us, event | category | flops | bytes accessed | tf_op | source)
XLA Modules:
  0.0 184.7 jit_solution(6500169789954286575)
XLA Ops:
  0.7 173.4 %layer.1 = (bf16[2,256,768]{2,1,0:T(8,128)(2,1)}, bf16[2,256,768]{2,1,0:T(8,128)(2,1)}, bf16[1536,768]{1,0:T(8,128)(2,1)}, bf16[768,1536]{1,0:T(8,128)(2,1)}, bf...) custom-call(bf16[2,256,768]{2,1,0:T(8,128)(2,1)} %x_in.1, bf16[2,256,768]{2,1,0:T(8,128)(2,1)} %cot_in.1, ...), custom_call_target="tpu_custom_call" | custom-call | flops 12000000000 | bytes 40000000 | tf_op jit(solution)/shard_map/layer/pallas_call | solution.py:893
  174.1 10.5 %widen.1 = (bf16[2,256,768]{2,1,0:T(8,128)(2,1)}, bf16[2,256,768]{2,1,0:T(8,128)(2,1)}, f32[1536,768]{1,0:T(8,128)}, f32[768,1536]{1,0:T(8,128)}, f32[3,768,384]...) custom-call(bf16[1536,768]{1,0:T(8,128)(2,1)} %get-tuple-element.35., ...), custom_call_target="tpu_custom_call" | custom-call | tf_op jit(solution)/shard_map/widen/pallas_call | solution.py:934

commit v3 on v2

--- a/solution.py
+++ b/solution.py
@@ -18,7 +18,17 @@
 SHORT, LONG = 0, 1
 ROOT = math.sqrt(2.0 / math.pi)
 CUBIC = 0.044715
-COPIES = 96
+COPIES = 112
+TAIL = (
+    *("feed_long", "post_long", "back_b", "b0", "in_d", "d0", "in_c", "b1", "back_a", "d1"),
+    *("c0", "c1", "post_short", "norm_long", "a0", "long3", "d2", "b2", "long1", "long2"),
+    *("long0", "b3", "a1", "norm_short", "short_back", "c2", "d3", "query_e", "bt", "hop"),
+    *("e0", "e1", "c3", "a2", "short_done", "long_done", "part_short", "br2", "pair_f", "part_long"),
+    *("ct", "f0", "vec_v", "a3", "v0", "e2", "v1", "f1", "cr2", "v2"),
+    *("e3", "br1", "v3", "f2", "cr1", "vt", "at", "done_long", "et", "vr2"),
+    *("f3", "ar2", "cr0", "er2", "vr1", "dt", "ft", "ar1", "done_short", "dr2"),
+    *("er1", "fr2", "dr1", "fr1", "br0", "er0", "ar0", "dr0", "fr0", "vr0"),
+)
 VEC_ROWS = 256
 
 
@@ -151,17 +161,25 @@
     gain_two_in,
     bias_two_in,
     in_bias_in,
+    short_len_in,
+    long_len_in,
+    short_table_in,
+    long_table_in,
+    out_in,
+    in_grad_in,
+    sum_back_a,
+    sum_back_b,
+    sum_in_a,
+    sum_in_b,
+    sum_query,
+    sum_pair,
+    sum_vec,
     short_len,
     long_len,
     short_table,
     long_table,
     out,
     in_grad,
-    sum_back,
-    sum_in,
-    sum_query,
-    sum_pair,
-    sum_vec,
     x,
     cot,
     qkvw,
@@ -200,14 +218,18 @@
     got_core,
     got_far,
     grad_proj,
-    part_back,
-    part_in,
+    part_back_a,
+    part_back_b,
+    part_in_a,
+    part_in_b,
     part_query,
     part_pair,
     part_vec,
     vec,
-    got_back,
-    got_in,
+    got_back_a,
+    got_back_b,
+    got_in_a,
+    got_in_b,
     got_query,
     got_pair,
     got_vec,
@@ -215,10 +237,10 @@
 ):
     upper = [16 << i for i in range(max(0, seq_count.bit_length() - 5))]
     if upper:
-        ups = rest[:5]
-        rest = rest[5:]
+        ups = rest[:7]
+        rest = rest[7:]
     else:
-        ups = (None,) * 5
+        ups = (None,) * 7
     send_sem, recv_sem, load_sem, local_sem = rest
     seq, head = lax.axis_index("seq"), lax.axis_index("head")
     links = Links(send_sem, recv_sem, seq, head)
@@ -240,16 +262,22 @@
 
     loads = []
     for i, (src, dst) in enumerate(
-        ((x_in, x), (qkvw_in, qkvw), (outw_in, outw), (win_in, win), (wout_in, wout), (cot_in, cot))
+        (
+            (x_in, x),
+            (qkvw_in, qkvw),
+            (short_len_in, short_len),
+            (long_len_in, long_len),
+            (short_table_in, short_table),
+            (long_table_in, long_table),
+            (outw_in, outw),
+            (win_in, win),
+            (wout_in, wout),
+            (cot_in, cot),
+        )
     ):
-        item = pltpu.make_async_copy(src, dst, load_sem.at[i])
+        loads.append(pltpu.make_async_copy(src, dst, load_sem.at[i]))
+    for item in loads[:6]:
         item.start()
-        loads.append(item)
-
-    vectors = (out_bias_in, gain_one_in, bias_one_in, back_bias_in, gain_two_in, bias_two_in)
-    for i, vector in enumerate(vectors):
-        params[i : i + 1, :wide] = vector[...].reshape(1, wide)
-    params[6:7, :] = in_bias_in[...].reshape(1, ff)
 
     def param(index):
         return params[index : index + 1, :wide]
@@ -259,7 +287,6 @@
     def tokens(mb):
         return pl.ds(mb * tok, tok)
 
-    vec[...] = jnp.zeros_like(vec)
     loads[0].wait()
     loads[1].wait()
 
@@ -268,22 +295,6 @@
 
     place = seq & (long_span - 1)
     side = seq & (short_span - 1)
-    kv_long[0, place] = project(LONG, 1).astype(BF16)
-    kv_long[1, place] = (project(LONG, 2) + qv_bias[1:2, :]).astype(BF16)
-    pl.semaphore_wait(barrier, len(peers) + 1)
-
-    def block(which, spot):
-        return kv_long.at[which, spot]
-
-    key_next = links.copy(block(0, place), block(0, place), 2)
-    value_far = links.copy(block(1, place), block(1, place), 4)
-    value_next = links.copy(block(1, place), block(1, place), 2)
-    key_far = links.copy(block(0, place), block(0, place), 4)
-    long_core = links.copy(kv_long.at[:, place], kv_long.at[:, place], 1)
-    kv_short[0, side] = project(SHORT, 1).astype(BF16)
-    kv_short[1, side] = (project(SHORT, 2) + qv_bias[1:2, :]).astype(BF16)
-    short_core = links.copy(kv_short.at[:, side], kv_short.at[:, side], 1)
-
     def spread_cols(pair):
         zero = jnp.zeros((HDIM, tok), BF16)
         return jnp.concatenate(
@@ -300,7 +311,7 @@
             [jnp.where(lane < HDIM, pair, 0.0), jnp.where(lane < HDIM, 0.0, pair)], 0
         ).astype(BF16)
 
-    for mb in (SHORT, LONG):
+    def queries(mb):
         query = (project(mb, 0) + qv_bias[0:1, :]).astype(BF16).astype(F32) * (HDIM**-0.5)
         for g in range(pairs):
             pair = query[:, g * 128 : g * 128 + 128]
@@ -327,8 +338,28 @@
 
         loop(count, step)
 
+    kv_long[0, place] = project(LONG, 1).astype(BF16)
+    kv_long[1, place] = (project(LONG, 2) + qv_bias[1:2, :]).astype(BF16)
+    kv_short[0, side] = project(SHORT, 1).astype(BF16)
+    kv_short[1, side] = (project(SHORT, 2) + qv_bias[1:2, :]).astype(BF16)
+    queries(SHORT)
+    for item in loads[2:6]:
+        item.wait()
     make_live(live_short, short_span, side, short_table, short_len[seq // short_span])
-    make_live(live_long, long_span, place, long_table, long_len[seq // long_span])
+    queries(LONG)
+
+    def block(which, spot):
+        return kv_long.at[which, spot]
+
+    pl.semaphore_wait(barrier, len(peers) + 1)
+    key_next = links.copy(block(0, place), block(0, place), 2)
+    value_far = links.copy(block(1, place), block(1, place), 4)
+    short_core = links.copy(kv_short.at[:, side], kv_short.at[:, side], 1)
+    long_core = links.copy(kv_long.at[:, place], kv_long.at[:, place], 1)
+    value_next = links.copy(block(1, place), block(1, place), 2)
+    key_far = links.copy(block(0, place), block(0, place), 4)
+    for item in loads[6:]:
+        item.start()
 
     def attend(mb, kv, live, spots, first=False):
         def pair_step(g):
@@ -376,6 +407,12 @@
         return post_out[buf, mb, rows, :].astype(F32) + post_in[buf, mb, rows, :].astype(F32)
 
     posts = {}
+    stores = []
+
+    def store(src, dst):
+        item = pltpu.make_async_copy(src, dst, load_sem.at[len(loads) + len(stores)])
+        item.start()
+        stores.append(item)
 
     def attention_out(mb):
         for g in range(pairs):
@@ -398,8 +435,15 @@
 
     short_core.wait()
     attend(SHORT, kv_short, live_short, tuple(range(short_span)), True)
-    loads[2].wait()
+    loads[6].wait()
     attention_out(SHORT)
+
+    make_live(live_long, long_span, place, long_table, long_len[seq // long_span])
+    vec[...] = jnp.zeros_like(vec)
+    vectors = (out_bias_in, gain_one_in, bias_one_in, back_bias_in, gain_two_in, bias_two_in)
+    for i, vector in enumerate(vectors):
+        params[i : i + 1, :wide] = vector[...].reshape(1, wide)
+    params[6:7, :] = in_bias_in[...].reshape(1, ff)
 
     key_next.wait_recv()
     key_corner = links.copy(block(0, place ^ 2), block(0, place ^ 2), 4)
@@ -415,6 +459,47 @@
     pass_next.wait_recv()
     pass_far.wait_recv()
     attend(LONG, kv_long, live_long, (place ^ 3, place ^ 5))
+
+    def mean(value):
+        return jnp.sum(value, axis=-1, keepdims=True) * (1.0 / wide)
+
+    def vec_add(index, value):
+        vec[index : index + 1, :wide] += jnp.sum(value, axis=0, keepdims=True)
+
+    tile_rows = 64
+
+    def feed_forward(mb):
+        posts[0, mb].wait_recv()
+        if mb == SHORT:
+            posts[0, mb].wait_send()
+
+        def norm_step(r):
+            rows = aligned(r * tile_rows, tile_rows, tile_rows)
+            joined = received(0, mb, rows) + param(OUTB) + x[mb, rows, :].astype(F32)
+            centred = joined - mean(joined)
+            root = lax.rsqrt(mean(centred * centred) + EPSILON)
+            normed = centred * root
+            norm_one[mb, rows, :] = normed
+            root_one[mb, rows, :] = jnp.broadcast_to(root, (tile_rows, 128))
+            all_rows = aligned(mb * tok + r * tile_rows, tile_rows, tile_rows)
+            hidden[all_rows, :] = (normed * param(GAIN1) + param(BIAS1)).astype(BF16)
+
+        loop(tok // tile_rows, norm_step)
+
+        def col_step(j):
+            lanes = aligned(j * 512, 512, 512)
+            u = dot(hidden[tokens(mb), :], win[:, lanes]) + params[6:7, lanes]
+            square = u * u
+            t = jnp.tanh(ROOT * u * (1.0 + CUBIC * square))
+            half = 0.5 * (1.0 + t)
+            act[tokens(mb), lanes] = (u * half).astype(BF16)
+            slope[mb, :, lanes] = half + (0.5 * ROOT) * u * (1.0 - t * t) * (
+                1.0 + (3.0 * CUBIC) * square
+            )
+
+        loop(ff // 512, col_step)
+        post_out[1, mb] = dot(act[tokens(mb), :], wout[...]).astype(BF16)
+
     key_corner.wait_recv()
     value_corner.wait_recv()
     pass_corner = links.copy(kv_long.at[:, place ^ 6], kv_long.at[:, place ^ 6], 1)
@@ -427,51 +512,13 @@
         pass_next, pass_far, pass_corner,
     ):
         item.wait_send()
-
-    def mean(value):
-        return jnp.sum(value, axis=-1, keepdims=True) * (1.0 / wide)
-
-    def vec_add(index, value):
-        vec[index : index + 1, :wide] += jnp.sum(value, axis=0, keepdims=True)
-
-    tile_rows = 64
-
-    def feed_forward(mb):
-        posts[0, mb].wait()
-
-        def norm_step(r):
-            rows = aligned(r * tile_rows, tile_rows, tile_rows)
-            joined = received(0, mb, rows) + param(OUTB) + x[mb, rows, :].astype(F32)
-            centred = joined - mean(joined)
-            root = lax.rsqrt(mean(centred * centred) + EPSILON)
-            normed = centred * root
-            norm_one[mb, rows, :] = normed
-            root_one[mb, rows, :] = jnp.broadcast_to(root, (tile_rows, 128))
-            all_rows = aligned(mb * tok + r * tile_rows, tile_rows, tile_rows)
-            hidden[all_rows, :] = (normed * param(GAIN1) + param(BIAS1)).astype(BF16)
-
-        loop(tok // tile_rows, norm_step)
-
-        def col_step(j):
-            lanes = aligned(j * 512, 512, 512)
-            u = dot(hidden[tokens(mb), :], win[:, lanes]) + params[6:7, lanes]
-            square = u * u
-            t = jnp.tanh(ROOT * u * (1.0 + CUBIC * square))
-            half = 0.5 * (1.0 + t)
-            act[tokens(mb), lanes] = (u * half).astype(BF16)
-            slope[mb, :, lanes] = half + (0.5 * ROOT) * u * (1.0 - t * t) * (
-                1.0 + (3.0 * CUBIC) * square
-            )
-
-        loop(ff // 512, col_step)
-        post_out[1, mb] = dot(act[tokens(mb), :], wout[...]).astype(BF16)
-        posts[1, mb] = post(1, mb)
-
-    loads[3].wait()
-    loads[4].wait()
-    loads[5].wait()
+    for item in loads[7:]:
+        item.wait()
     feed_forward(SHORT)
+    posts[0, LONG].wait_send()
+    posts[1, SHORT] = post(1, SHORT)
     feed_forward(LONG)
+    posts[1, LONG] = post(1, LONG)
 
     def norm_back(grad, normed, root):
         return root * (grad - mean(grad) - normed * mean(grad * normed))
@@ -497,6 +544,7 @@
             grad_feed[all_rows, :] = grad.astype(BF16)
 
         loop(tok // tile_rows, norm_step)
+        store(out.at[mb], out_in.at[mb])
 
     def feed_back(mb):
         def col_step(j):
@@ -508,38 +556,41 @@
 
         loop(ff // 512, col_step)
         post_out[0, mb] = dot(grad_inner[tokens(mb), :], win[...], 1, 1).astype(BF16)
-        posts[2, mb] = post(2, mb)
 
     feed_norm(SHORT)
     feed_back(SHORT)
 
+    feed_norm(LONG)
+
     def reduction(index, part, total, got, order):
         return Reduction(links, part, total, got, order, ups[index], upper, local_sem.at[index])
 
     near_first, far_first = (1, 2, 4, 8), (1, 4, 8, 2)
-    red_back = reduction(0, part_back, sum_back, got_back, near_first)
-    red_in = reduction(1, part_in, sum_in, got_in, near_first)
-    red_query = reduction(2, part_query, sum_query, got_query, far_first)
-    red_pair = reduction(3, part_pair, sum_pair, got_pair, near_first)
-    red_vec = reduction(4, part_vec, sum_vec, got_vec, near_first)
-
-    feed_norm(LONG)
-
-    def back_step(j):
-        rows = aligned(j * 256, 256, 256)
-        part_back[rows, :] = dot(act[:, rows], grad_feed[...], 0, 0).astype(BF16)
-
-    loop(ff // 256, back_step)
-    red_back.step(0)
-    feed_back(LONG)
-
-    def in_step(j):
-        rows = aligned(j * 256, 256, 256)
-        part_in[rows, :] = dot(hidden[:, rows], grad_inner[...], 0, 0).astype(BF16)
-
-    red_back.step(1)
-    loop(wide // 256, in_step)
-    red_in.step(0)
+    red = {
+        "a": reduction(0, part_back_a, sum_back_a, got_back_a, near_first),
+        "b": reduction(1, part_back_b, sum_back_b, got_back_b, near_first),
+        "c": reduction(2, part_in_a, sum_in_a, got_in_a, near_first),
+        "d": reduction(3, part_in_b, sum_in_b, got_in_b, far_first),
+        "e": reduction(4, part_query, sum_query, got_query, near_first),
+        "f": reduction(5, part_pair, sum_pair, got_pair, near_first),
+        "v": reduction(6, part_vec, sum_vec, got_vec, near_first),
+    }
+
+    def back_grad(part, start):
+        def step(j):
+            rows = aligned(j * 256, 256, 256)
+            lanes = aligned(start + j * 256, 256, 256)
+            part[rows, :] = dot(act[:, lanes], grad_feed[...], 0, 0).astype(BF16)
+
+        loop(ff // 512, step)
+
+    def in_grad_half(part, start):
+        def step(j):
+            rows = aligned(j * 256, 256, 256)
+            inner = grad_inner[:, start : start + ff // 2]
+            part[rows, :] = dot(hidden[:, rows], inner, 0, 0).astype(BF16)
+
+        loop(wide // 256, step)
 
     def norm_one_back(mb):
         posts[2, mb].wait()
@@ -614,14 +665,6 @@
 
         return store
 
-    norm_one_back(SHORT)
-    attend_back(SHORT, kv_short, live_short, 1 - side, store_short(1 - side), True)
-    short_grads = links.copy(dkv_short.at[:, 1 - side], got_short, 1)
-    attend_back(SHORT, kv_short, live_short, side, store_short(side))
-    query_done(SHORT)
-    red_in.step(1)
-    red_back.step(2)
-    norm_one_back(LONG)
     mine = (seq >> 1) & 3
 
     def add_block(which, j, more):
@@ -635,9 +678,10 @@
     core_grads = []
     key_hop = []
     value_hop = []
-    for order, d in enumerate((3, 1, 2, 0)):
+
+    def long_back(d):
         j = mine ^ d
-        attend_back(LONG, kv_long, live_long, 2 * j + 1 - core, store_long(j, 1 - core), order == 0)
+        attend_back(LONG, kv_long, live_long, 2 * j + 1 - core, store_long(j, 1 - core), d == 3)
         item = links.copy(dkv_long.at[:, j, 1 - core], got_core.at[:, j], 1)
         core_grads.append(item)
         attend_back(LONG, kv_long, live_long, 2 * j + core, store_long(j, core))
@@ -645,16 +689,19 @@
         for which in range(2):
             add_block(which, j, got_core.at[which, j])
         if d == 1:
-            key_hop = [go_far(0, mine ^ 3, 0, 2), go_far(0, mine ^ 1, 1, 2)]
+            key_hop.extend([go_far(0, mine ^ 3, 0, 2), go_far(0, mine ^ 1, 1, 2)])
         if d == 2:
-            value_hop = [go_far(1, mine ^ 3, 2, 4), go_far(1, mine ^ 2, 3, 4)]
-    query_done(LONG)
-    key_hop[0].wait_recv()
-    add_block(0, mine ^ 2, got_far.at[0])
-    key_hop.append(go_far(0, mine ^ 2, 4, 4))
-    value_hop[0].wait_recv()
-    add_block(1, mine ^ 1, got_far.at[2])
-    value_hop.append(go_far(1, mine ^ 1, 5, 2))
+            value_hop.extend([go_far(1, mine ^ 3, 2, 4), go_far(1, mine ^ 2, 3, 4)])
+        if d == 0:
+            query_done(LONG)
+
+    def second_hop():
+        key_hop[0].wait_recv()
+        add_block(0, mine ^ 2, got_far.at[0])
+        key_hop.append(go_far(0, mine ^ 2, 4, 4))
+        value_hop[0].wait_recv()
+        add_block(1, mine ^ 1, got_far.at[2])
+        value_hop.append(go_far(1, mine ^ 1, 5, 2))
 
     half_wide = wide // 2
 
@@ -662,8 +709,6 @@
         lanes = aligned(j * half_wide, half_wide, half_wide)
         rows = aligned(j * col, col, col)
         part_query[rows, 0:col] = dot(mixed[...], grad_attn[:, lanes], 0, 0).astype(BF16)
-
-    loop(2, out_step)
 
     def x_grad(items):
         def step(j):
@@ -673,15 +718,6 @@
                 part[rows, lanes] = dot(columns, grad_proj[:, source], 0, 0).astype(BF16)
 
         loop(wide // 256, step)
-
-    x_grad([(part_query, slice(col, 2 * col), slice(0, col))])
-    red_query.step(0)
-
-    short_grads.wait()
-    for which in range(2):
-        lanes = slice((1 + which) * col, (2 + which) * col)
-        total = dkv_short[which, side].astype(F32) + got_short[which].astype(F32)
-        grad_proj[tokens(SHORT), lanes] = total.astype(BF16)
 
     def input_part(mb):
         rows = tokens(mb)
@@ -699,87 +735,114 @@
             in_grad[mb, rows, :] = (grad_rows[mb, rows, :] + received(3, mb, rows)).astype(BF16)
 
         loop(tok // tile_rows, step)
-
-    input_part(SHORT)
-    red_in.step(2)
-    red_back.step(3)
-    red_query.step(1)
-
-    for hop, which in ((key_hop, 0), (value_hop, 1)):
-        lanes = slice((1 + which) * col, (2 + which) * col)
-        hop[1].wait_recv()
-        hop[2].wait_recv()
-        total = dkv_long[which, mine, core].astype(F32) + got_far[2 * which + 1].astype(F32)
-        total = total + got_far[4 + which].astype(F32)
-        grad_proj[tokens(LONG), lanes] = total.astype(BF16)
-    x_grad(
-        [
-            (part_pair, slice(0, col), slice(col, 2 * col)),
-            (part_pair, slice(col, 2 * col), slice(2 * col, 3 * col)),
-        ]
-    )
-    red_pair.step(0)
-
-    vec[7:8, 0:col] = jnp.sum(grad_proj[:, 0:col].astype(F32), axis=0, keepdims=True)
-    vec[7:8, col : 2 * col] = jnp.sum(
-        grad_proj[:, 2 * col : 3 * col].astype(F32), axis=0, keepdims=True
-    )
-    part_vec[...] = jnp.zeros_like(part_vec)
-    lines = []
-    for index, width in [(i, wide) for i in range(6)] + [(7, 2 * col), (6, ff)]:
-        for k in range(width // 128):
-            lines.append(vec[index : index + 1, k * 128 : k * 128 + 128])
-    while len(lines) % 16:
-        lines.append(jnp.zeros((1, 128), F32))
-    part_vec[0 : len(lines), :] = jnp.concatenate(lines, 0).astype(BF16)
-    red_vec.step(0)
-    input_part(LONG)
-
-    red_back.total()
-    red_pair.step(1)
-    red_vec.step(1)
-    red_in.step(3)
-    red_query.step(2)
-    red_back.back(2)
-    input_done(SHORT)
-    red_in.total()
-    red_pair.step(2)
-    red_vec.step(2)
-    red_query.step(3)
-    red_back.back(1)
-    red_in.back(2)
-    red_pair.step(3)
-    red_vec.step(3)
-    red_query.total()
-    red_in.back(1)
-    red_pair.total()
-    red_vec.total()
-    red_query.back(2)
-    input_done(LONG)
-    red_pair.back(2)
-    red_vec.back(2)
-    red_back.back(0)
-    red_query.back(1)
-    red_pair.back(1)
-    red_vec.back(1)
-    red_in.back(0)
-    red_query.back(0)
-    red_pair.back(0)
-    red_vec.back(0)
-    for item in (red_back, red_in, red_query, red_pair, red_vec):
+        store(in_grad.at[mb], in_grad_in.at[mb])
+
+    short_grads = []
+
+    def short_back():
+        attend_back(SHORT, kv_short, live_short, 1 - side, store_short(1 - side), True)
+        short_grads.append(links.copy(dkv_short.at[:, 1 - side], got_short, 1))
+        attend_back(SHORT, kv_short, live_short, side, store_short(side))
+        query_done(SHORT)
+
+    def query_grad():
+        loop(2, out_step)
+        x_grad([(part_query, slice(col, 2 * col), slice(0, col))])
+
+    def short_done():
+        short_grads[0].wait()
+        for which in range(2):
+            lanes = slice((1 + which) * col, (2 + which) * col)
+            total = dkv_short[which, side].astype(F32) + got_short[which].astype(F32)
+            grad_proj[tokens(SHORT), lanes] = total.astype(BF16)
+
+    def long_done():
+        for hop, which in ((key_hop, 0), (value_hop, 1)):
+            lanes = slice((1 + which) * col, (2 + which) * col)
+            hop[1].wait_recv()
+            hop[2].wait_recv()
+            total = dkv_long[which, mine, core].astype(F32) + got_far[2 * which + 1].astype(F32)
+            total = total + got_far[4 + which].astype(F32)
+            grad_proj[tokens(LONG), lanes] = total.astype(BF16)
+
+    def pair_grad():
+        x_grad(
+            [
+                (part_pair, slice(0, col), slice(col, 2 * col)),
+                (part_pair, slice(col, 2 * col), slice(2 * col, 3 * col)),
+            ]
+        )
+
+    def vectors_done():
+        vec[7:8, 0:col] = jnp.sum(grad_proj[:, 0:col].astype(F32), axis=0, keepdims=True)
+        vec[7:8, col : 2 * col] = jnp.sum(
+            grad_proj[:, 2 * col : 3 * col].astype(F32), axis=0, keepdims=True
+        )
+        part_vec[...] = jnp.zeros_like(part_vec)
+        lines = []
+        for index, width in [(i, wide) for i in range(6)] + [(7, 2 * col), (6, ff)]:
+            for k in range(width // 128):
+                lines.append(vec[index : index + 1, k * 128 : k * 128 + 128])
+        while len(lines) % 16:
+            lines.append(jnp.zeros((1, 128), F32))
+        part_vec[0 : len(lines), :] = jnp.concatenate(lines, 0).astype(BF16)
+
+    def post_now(stage, mb):
+        posts[stage, mb] = post(stage, mb)
+
+    steps = {
+        "back_a": lambda: back_grad(part_back_a, 0),
+        "back_b": lambda: back_grad(part_back_b, ff // 2),
+        "feed_long": lambda: feed_back(LONG),
+        "post_long": lambda: post_now(2, LONG),
+        "in_c": lambda: in_grad_half(part_in_a, 0),
+        "in_d": lambda: in_grad_half(part_in_b, ff // 2),
+        "norm_long": lambda: norm_one_back(LONG),
+        "post_short": lambda: post_now(2, SHORT),
+        "long3": lambda: long_back(3),
+        "long1": lambda: long_back(1),
+        "long2": lambda: long_back(2),
+        "long0": lambda: long_back(0),
+        "hop": second_hop,
+        "norm_short": lambda: norm_one_back(SHORT),
+        "short_back": short_back,
+        "query_e": query_grad,
+        "short_done": short_done,
+        "part_short": lambda: input_part(SHORT),
+        "long_done": long_done,
+        "pair_f": pair_grad,
+        "vec_v": vectors_done,
+        "part_long": lambda: input_part(LONG),
+        "done_short": lambda: input_done(SHORT),
+        "done_long": lambda: input_done(LONG),
+    }
+    for name, item in red.items():
+        for i in range(4):
+            steps[name + str(i)] = functools.partial(item.step, i)
+        steps[name + "t"] = item.total
+        for i in range(3):
+            steps[name + "r" + str(i)] = functools.partial(item.back, i)
+    for name in TAIL:
+        steps[name]()
+    for item in red.values():
         item.finish()
     for item in core_grads + key_hop + value_hop:
         item.wait_send()
-
-
-def widen(back, inner, query, out_low, out_high, pair, vec, out_in, grad_in, *outs):
+    for item in stores:
+        item.wait()
+
+
+def widen(back_a, back_b, inner_a, inner_b, query, out_low, out_high, pair, vec, out_in, grad_in, *outs):
     out, in_grad, g_back, g_inner, g_qkv, g_out, g_qv, g_in_bias, *vectors = outs
     col = query.shape[1]
     wide = vectors[0].shape[0]
     out[...] = out_in[...]
     in_grad[...] = grad_in[...]
-    g_back[...] = back[...].astype(F32)
-    g_inner[...] = inner[...].astype(F32)
+    g_back[0] = back_a[...].astype(F32)
+    g_back[1] = back_b[...].astype(F32)
+    half = inner_a.shape[1]
+    g_inner[:, :half] = inner_a[...].astype(F32)
+    g_inner[:, half:] = inner_b[...].astype(F32)
     g_qkv[0] = query[...].astype(F32)
     g_qkv[1] = pair[:, :col].astype(F32)
     g_qkv[2] = pair[:, col:].astype(F32)
@@ -834,9 +897,15 @@
     long_span = seq_count // long_lengths.shape[0]
     upper = max(0, seq_count.bit_length() - 5)
 
-    parts = [(ff, wide), (wide, ff), (wide, 2 * col), (wide, 2 * col), (VEC_ROWS, 128)]
+    parts = [(ff // 2, wide)] * 2 + [(wide, ff // 2)] * 2 + [(wide, 2 * col)] * 2 + [(VEC_ROWS, 128)]
     vmem = pltpu.VMEM
     scratch = [
+        pltpu.SMEM(short_lengths.shape, jnp.int32),
+        pltpu.SMEM(long_lengths.shape, jnp.int32),
+        pltpu.SMEM(short_random.shape, jnp.int32),
+        pltpu.SMEM(long_random.shape, jnp.int32),
+        vmem((2, tok, wide), BF16),
+        vmem((2, tok, wide), BF16),
         vmem((2, tok, wide), BF16),
         vmem((2, tok, wide), BF16),
         vmem((3, wide, col), BF16),
@@ -884,21 +953,20 @@
     scratch += [
         pltpu.SemaphoreType.DMA((COPIES,)),
         pltpu.SemaphoreType.DMA((COPIES,)),
-        pltpu.SemaphoreType.DMA((8,)),
+        pltpu.SemaphoreType.DMA((16,)),
         pltpu.SemaphoreType.DMA((8,)),
     ]
     any_spec = pl.BlockSpec(memory_space=pl.ANY)
     vmem_spec = pl.BlockSpec(memory_space=pltpu.VMEM)
-    smem_spec = pl.BlockSpec(memory_space=pltpu.SMEM)
-    out, in_grad, s_back, s_in, s_query, s_pair, s_vec = pl.pallas_call(
+    out, in_grad, s_back_a, s_back_b, s_in_a, s_in_b, s_query, s_pair, s_vec = pl.pallas_call(
         functools.partial(kernel, seq_count),
         out_shape=[
             jax.ShapeDtypeStruct(inputs.shape, BF16),
             jax.ShapeDtypeStruct(inputs.shape, BF16),
         ]
         + [jax.ShapeDtypeStruct(shape, BF16) for shape in parts],
-        in_specs=[any_spec] * 6 + [vmem_spec] * 8 + [smem_spec] * 4,
-        out_specs=[vmem_spec] * 2 + [any_spec] * 5,
+        in_specs=[any_spec] * 6 + [vmem_spec] * 8 + [any_spec] * 4,
+        out_specs=[any_spec] * 9,
         scratch_shapes=scratch,
         compiler_params=pltpu.CompilerParams(
             collective_id=0, has_side_effects=True, vmem_limit_bytes=63 * 1024 * 1024
@@ -937,7 +1005,7 @@
         out_shape=[
             jax.ShapeDtypeStruct(inputs.shape, BF16),
             jax.ShapeDtypeStruct(inputs.shape, BF16),
-            jax.ShapeDtypeStruct((ff, wide), F32),
+            jax.ShapeDtypeStruct((2, ff // 2, wide), F32),
             jax.ShapeDtypeStruct((wide, ff), F32),
             jax.ShapeDtypeStruct((3, wide, col), F32),
             jax.ShapeDtypeStruct((col, wide), F32),
@@ -946,8 +1014,10 @@
         ]
         + [vector] * 6,
         in_specs=[
-            pl.BlockSpec((ff // steps, wide), lambda i: (i, 0)),
-            pl.BlockSpec((wide // steps, ff), lambda i: (i, 0)),
+            pl.BlockSpec((ff // 2 // steps, wide), lambda i: (i, 0)),
+            pl.BlockSpec((ff // 2 // steps, wide), lambda i: (i, 0)),
+            pl.BlockSpec((wide // steps, ff // 2), lambda i: (i, 0)),
+            pl.BlockSpec((wide // steps, ff // 2), lambda i: (i, 0)),
             pl.BlockSpec((wide // steps, col), lambda i: (i, 1)),
             pl.BlockSpec((col // steps, col), lambda i: (i, 0)),
             pl.BlockSpec((col // steps, col), lambda i: (i + steps, 0)),
@@ -959,7 +1029,7 @@
         out_specs=[
             rows_spec,
             rows_spec,
-            pl.BlockSpec((ff // steps, wide), lambda i: (i, 0)),
+            pl.BlockSpec((2, ff // 2 // steps, wide), lambda i: (0, i, 0)),
             pl.BlockSpec((wide // steps, ff), lambda i: (i, 0)),
             pl.BlockSpec((3, wide // steps, col), lambda i: (0, i, 0)),
             pl.BlockSpec((col // steps, wide), lambda i: (i, 0)),
@@ -967,7 +1037,7 @@
         + [whole] * 8,
         compiler_params=pltpu.CompilerParams(vmem_limit_bytes=63 * 1024 * 1024),
         name="widen",
-    )(s_back, s_in, s_query, s_query, s_query, s_pair, s_vec, out, in_grad)
+    )(s_back_a, s_back_b, s_in_a, s_in_b, s_query, s_query, s_query, s_pair, s_vec, out, in_grad)
     return (
         out,
         in_grad,
@@ -979,7 +1049,7 @@
         vectors[2],
         g_inner,
         g_in_bias,
-        g_back,
+        g_back.reshape(ff, wide),
         vectors[3],
         vectors[4],
         vectors[5],

time: 185 us -> 171 us (0.924)
  Pallas kernels: 184 us -> 169 us
    pallas_call x1, Pallas kernels: 173 us -> 159 us  [body(): pl.pallas_call(functools.partial(kernel, seq_count), out_shape=[jax.Shape...]
where the time goes in v3:
time: 171 us; the launch traced here: 170 us
  Pallas kernels  169 us (99%)
    pallas_call x1, Pallas kernels, body(): pl.pallas_call(functools.partial(kernel, seq_count), out_shape=[jax.Shape...  159 us
    pallas_call x1, Pallas kernels, body(): pl.pallas_call(widen, grid=(steps,), out_shape=[jax.ShapeDtypeStruct(inpu...  10.5 us

profile of v3, /device:TPU:0, one launch (start us, length us, event | category | flops | bytes accessed | tf_op | source)
XLA Modules:
  0.0 170.2 jit_solution(16079149243204581504)
XLA Ops:
  0.7 158.8 %layer.1 = (bf16[2,256,768]{2,1,0:T(8,128)(2,1)}, bf16[2,256,768]{2,1,0:T(8,128)(2,1)}, bf16[768,768]{1,0:T(8,128)(2,1)}, bf16[768,768]{1,0:T(8,128)(2,1)}, bf16...) custom-call(bf16[2,256,768]{2,1,0:T(8,128)(2,1)} %x_in.1, ...), custom_call_target="tpu_custom_call" | custom-call | flops 12000000000 | bytes 40000000 | tf_op jit(solution)/shard_map/layer/pallas_call | solution.py:961
  159.4 10.5 %widen.1 = (bf16[2,256,768]{2,1,0:T(8,128)(2,1)}, bf16[2,256,768]{2,1,0:T(8,128)(2,1)}, f32[2,768,768]{2,1,0:T(8,128)}, f32[768,1536]{1,0:T(8,128)}, f32[3,768,3...) custom-call(bf16[768,768]{1,0:T(8,128)(2,1)} %get-tuple-element.37.b, ...), custom_call_target="tpu_custom_call" | custom-call | tf_op jit(solution)/shard_map/widen/pallas_call | solution.py:1002

commit v4 on v3

--- a/solution.py
+++ b/solution.py
@@ -20,14 +20,15 @@
 CUBIC = 0.044715
 COPIES = 112
 TAIL = (
-    *("feed_long", "post_long", "back_b", "b0", "in_d", "d0", "in_c", "b1", "back_a", "d1"),
-    *("c0", "c1", "post_short", "norm_long", "a0", "long3", "d2", "b2", "long1", "long2"),
-    *("long0", "b3", "a1", "norm_short", "short_back", "c2", "d3", "query_e", "bt", "hop"),
-    *("e0", "e1", "c3", "a2", "short_done", "long_done", "part_short", "br2", "pair_f", "part_long"),
-    *("ct", "f0", "vec_v", "a3", "v0", "e2", "v1", "f1", "cr2", "v2"),
-    *("e3", "br1", "v3", "f2", "cr1", "vt", "at", "done_long", "et", "vr2"),
-    *("f3", "ar2", "cr0", "er2", "vr1", "dt", "ft", "ar1", "done_short", "dr2"),
-    *("er1", "fr2", "dr1", "fr1", "br0", "er0", "ar0", "dr0", "fr0", "vr0"),
+    *("feed_long", "post_long", "back_b", "b0", "in_c", "c0", "in_d", "b1", "back_a", "c1"),
+    *("a0", "a1", "d0", "norm_long", "long3", "b2", "post_short", "c2", "long1", "a2"),
+    *("long2", "d1", "long0", "norm_short", "short_back", "short_done", "a3", "hop", "query_e", "e0"),
+    *("at", "part_short", "d2", "e1", "long_done", "b3", "pair_f", "vec_v", "f0", "ar2"),
+    *("v0", "d3", "f1", "e2", "v1", "bt", "dt", "ar1", "c3", "f2"),
+    *("e3", "br2", "ct", "f3", "v2", "done_short", "et", "dr2", "br1", "ft"),
+    *("er2", "dr1", "v3", "part_long", "cr2", "er1", "fr2", "cr1", "br0", "done_long"),
+    *("fr1", "vt", "dr0", "vr2", "er0", "cr0", "bs", "ar0", "ds", "vr1"),
+    *("fr0", "es", "vr0", "cs", "as", "fs", "vs"),
 )
 VEC_ROWS = 256
 
@@ -78,8 +79,9 @@
 
 
 class Reduction:
-    def __init__(self, links, part, out, got, deltas, up, upper, local_sem):
+    def __init__(self, links, part, out, full, got, deltas, up, upper, local_sem):
         self.links, self.part, self.out, self.got = links, part, out, got
+        self.full = full
         self.up, self.upper, self.local_sem = up, upper, local_sem
         self.deltas = deltas
         size = part.shape[0]
@@ -126,21 +128,28 @@
             item = self.links.copy(mine, self.up.at[level], delta)
             item.wait()
             add_rows(self.part, self.share_at, self.up.at[level], 0, self.share, self.tile)
-        there = self.rows(self.out, self.share_at, self.share)
-        self.go(mine, there, self.deltas[-1])
-        self.kept = pltpu.make_async_copy(mine, there, self.local_sem)
-        self.kept.start()
+        ready = self.rows(self.full, self.share_at, self.share)
+
+        def step(i):
+            rows = aligned(self.share_at + i * self.tile, self.tile, 16)
+            self.full[rows, :] = self.part[rows, :]
+
+        loop(self.share // self.tile, step)
+        self.go(ready, ready, self.deltas[-1])
 
     def back(self, index):
         self.last.wait_recv()
-        if index == len(self.levels) - 2:
-            self.kept.wait()
         delta, size, start, kept, away, got_at = self.levels[index]
-        block = self.rows(self.out, kept, size)
+        block = self.rows(self.full, kept, size)
         self.go(block, block, delta)
 
+    def keep(self):
+        self.last.wait_recv()
+        self.kept = pltpu.make_async_copy(self.full, self.out, self.local_sem)
+        self.kept.start()
+
     def finish(self):
-        self.last.wait_recv()
+        self.kept.wait()
         for item in self.sent:
             item.wait_send()
 
@@ -179,7 +188,6 @@
     short_table,
     long_table,
     out,
-    in_grad,
     x,
     cot,
     qkvw,
@@ -241,7 +249,7 @@
         rest = rest[7:]
     else:
         ups = (None,) * 7
-    send_sem, recv_sem, load_sem, local_sem = rest
+    fulls, (send_sem, recv_sem, load_sem, local_sem) = rest[:7], rest[7:]
     seq, head = lax.axis_index("seq"), lax.axis_index("head")
     links = Links(send_sem, recv_sem, seq, head)
     tok = x.shape[1]
@@ -356,12 +364,10 @@
     value_far = links.copy(block(1, place), block(1, place), 4)
     short_core = links.copy(kv_short.at[:, side], kv_short.at[:, side], 1)
     long_core = links.copy(kv_long.at[:, place], kv_long.at[:, place], 1)
-    value_next = links.copy(block(1, place), block(1, place), 2)
-    key_far = links.copy(block(0, place), block(0, place), 4)
     for item in loads[6:]:
         item.start()
 
-    def attend(mb, kv, live, spots, first=False):
+    def attend(mb, kv, live, spots, first=False, low=0, high=pairs):
         def pair_step(g):
             lanes = aligned(g * 128, 128, 128)
             q2 = q_cols[mb, g]
@@ -396,7 +402,7 @@
             mixed_cols[mb, rows_a, :] = acc_a
             mixed_cols[mb, rows_b, :] = acc_b
 
-        loop(pairs, pair_step)
+        loop(high - low, lambda g: pair_step(g + low))
 
     def post(stage, mb):
         buf = stage % 2
@@ -434,7 +440,13 @@
         posts[0, mb] = post(0, mb)
 
     short_core.wait()
-    attend(SHORT, kv_short, live_short, tuple(range(short_span)), True)
+    short_spots = tuple(range(short_span))
+    attend(SHORT, kv_short, live_short, short_spots, True, 0, pairs - 1)
+    key_next.wait_send()
+    value_far.wait_send()
+    value_next = links.copy(block(1, place), block(1, place), 2)
+    key_far = links.copy(block(0, place), block(0, place), 4)
+    attend(SHORT, kv_short, live_short, short_spots, True, pairs - 1, pairs)
     loads[6].wait()
     attention_out(SHORT)
 
@@ -493,9 +505,9 @@
             t = jnp.tanh(ROOT * u * (1.0 + CUBIC * square))
             half = 0.5 * (1.0 + t)
             act[tokens(mb), lanes] = (u * half).astype(BF16)
-            slope[mb, :, lanes] = half + (0.5 * ROOT) * u * (1.0 - t * t) * (
-                1.0 + (3.0 * CUBIC) * square
-            )
+            slope[mb, :, lanes] = (
+                half + (0.5 * ROOT) * u * (1.0 - t * t) * (1.0 + (3.0 * CUBIC) * square)
+            ).astype(BF16)
 
         loop(ff // 512, col_step)
         post_out[1, mb] = dot(act[tokens(mb), :], wout[...]).astype(BF16)
@@ -508,7 +520,7 @@
     attend(LONG, kv_long, live_long, (place ^ 7,))
     attention_out(LONG)
     for item in (
-        key_next, value_far, value_next, key_far, key_corner, value_corner,
+        value_next, key_far, key_corner, value_corner,
         pass_next, pass_far, pass_corner,
     ):
         item.wait_send()
@@ -550,7 +562,7 @@
         def col_step(j):
             lanes = aligned(j * 512, 512, 512)
             grad_act = dot(grad_feed[tokens(mb), :], wout[lanes, :], 1, 1).astype(BF16)
-            low = (grad_act.astype(F32) * slope[mb, :, lanes]).astype(BF16)
+            low = (grad_act.astype(F32) * slope[mb, :, lanes].astype(F32)).astype(BF16)
             grad_inner[tokens(mb), lanes] = low
             vec[6:7, lanes] += jnp.sum(low.astype(F32), axis=0, keepdims=True)
 
@@ -563,14 +575,14 @@
     feed_norm(LONG)
 
     def reduction(index, part, total, got, order):
-        return Reduction(links, part, total, got, order, ups[index], upper, local_sem.at[index])
+        return Reduction(links, part, total, fulls[index], got, order, ups[index], upper, local_sem.at[index])
 
     near_first, far_first = (1, 2, 4, 8), (1, 4, 8, 2)
     red = {
         "a": reduction(0, part_back_a, sum_back_a, got_back_a, near_first),
         "b": reduction(1, part_back_b, sum_back_b, got_back_b, near_first),
-        "c": reduction(2, part_in_a, sum_in_a, got_in_a, near_first),
-        "d": reduction(3, part_in_b, sum_in_b, got_in_b, far_first),
+        "c": reduction(2, part_in_a, sum_in_a, got_in_a, far_first),
+        "d": reduction(3, part_in_b, sum_in_b, got_in_b, near_first),
         "e": reduction(4, part_query, sum_query, got_query, near_first),
         "f": reduction(5, part_pair, sum_pair, got_pair, near_first),
         "v": reduction(6, part_vec, sum_vec, got_vec, near_first),
@@ -729,13 +741,14 @@
 
     def input_done(mb):
         posts[3, mb].wait()
+        stores[mb].wait()
 
         def step(r):
             rows = aligned(r * tile_rows, tile_rows, tile_rows)
-            in_grad[mb, rows, :] = (grad_rows[mb, rows, :] + received(3, mb, rows)).astype(BF16)
+            out[mb, rows, :] = (grad_rows[mb, rows, :] + received(3, mb, rows)).astype(BF16)
 
         loop(tok // tile_rows, step)
-        store(in_grad.at[mb], in_grad_in.at[mb])
+        store(out.at[mb], in_grad_in.at[mb])
 
     short_grads = []
 
@@ -820,6 +833,7 @@
         for i in range(4):
             steps[name + str(i)] = functools.partial(item.step, i)
         steps[name + "t"] = item.total
+        steps[name + "s"] = item.keep
         for i in range(3):
             steps[name + "r" + str(i)] = functools.partial(item.back, i)
     for name in TAIL:
@@ -828,44 +842,116 @@
         item.finish()
     for item in core_grads + key_hop + value_hop:
         item.wait_send()
+    for item in stores[2:]:
+        item.wait()
+
+
+def widen(
+    sum_back_a,
+    sum_back_b,
+    sum_in_a,
+    sum_in_b,
+    sum_query,
+    sum_pair,
+    sum_vec,
+    out_in,
+    grad_in,
+    out,
+    in_grad,
+    g_back,
+    g_inner,
+    g_qkv,
+    g_out,
+    g_qv,
+    g_in_bias,
+    *rest,
+):
+    vectors = rest[:6]
+    lows, highs, load_sem, store_sem, copy_sem = rest[6:11], rest[11:15], *rest[15:18]
+    low_back, low_in, low_query, low_pair, low_vec = lows
+    high_back, high_in, high_qkv, high_out = highs
+    col = sum_query.shape[1] // 2
+    wide = sum_query.shape[0]
+    low_out, low_grad = rest[18:20]
+    copies = [
+        pltpu.make_async_copy(out_in, low_out, copy_sem.at[0]),
+        pltpu.make_async_copy(grad_in, low_grad, copy_sem.at[1]),
+    ]
+    loads = {}
+    half = wide // 2
+
+    def load(name, src, dst):
+        loads[name] = pltpu.make_async_copy(src, dst, load_sem.at[len(loads)])
+        loads[name].start()
+
+    first, second = pl.ds(0, half), pl.ds(half, half)
+    load("vec", sum_vec, low_vec)
+    load("query", sum_query, low_query)
+    for part, name in ((first, "0"), (second, "1")):
+        load("pair" + name, sum_pair.at[part], low_pair.at[part])
+    for i, (back, inner) in enumerate(((sum_back_a, sum_in_a), (sum_back_b, sum_in_b))):
+        for part, name in ((first, "0"), (second, "1")):
+            load("back" + str(i) + name, back.at[part], low_back.at[i, part])
+            load("in" + str(i) + name, inner.at[part], low_in.at[i, part])
+    for item in copies:
+        item.start()
+    stores = []
+
+    def store(src, dst):
+        item = pltpu.make_async_copy(src, dst, store_sem.at[len(stores)])
+        item.start()
+        stores.append(item)
+
+    def cast(dst, src, start, rows, lanes, src_lanes, src_start=None):
+        shift = 0 if src_start is None else src_start - start
+
+        def step(r):
+            here = aligned(start + r * 32, 32, 32)
+            there = aligned(start + shift + r * 32, 32, 32)
+            dst[here, lanes] = src[there, src_lanes].astype(F32)
+
+        loop(rows // 32, step)
+
+    for item, low, high in zip(copies, (low_out, low_grad), (out, in_grad)):
+        item.wait()
+        store(low, high)
+    loads["vec"].wait()
+    full = low_vec[...].astype(F32)
+
+    def line(row, count):
+        return jnp.concatenate([full[r : r + 1, :] for r in range(row, row + count)], 1)
+
+    per = wide // 128
+    for i, vector in enumerate(vectors):
+        vector[...] = line(i * per, per).reshape(wide)
+    row = len(vectors) * per
+    g_qv[...] = jnp.concatenate([line(row, col // 128), line(row + col // 128, col // 128)], 0)
+    bias = line(row + 2 * col // 128, g_in_bias.shape[0] // 128)
+    g_in_bias[...] = bias.reshape(g_in_bias.shape[0])
+    left, right, every = pl.ds(0, col), pl.ds(col, col), slice(None)
+    loads["query"].wait()
+    cast(high_out, low_query, 0, col, left, left)
+    cast(high_out, low_query, 0, col, right, left, col)
+    store(high_out, g_out)
+    cast(high_qkv.at[0], low_query, 0, wide, every, right)
+    store(high_qkv.at[0], g_qkv.at[0])
+    for part, name, start in ((first, "0", 0), (second, "1", half)):
+        loads["pair" + name].wait()
+        cast(high_qkv.at[1], low_pair, start, half, every, left)
+        cast(high_qkv.at[2], low_pair, start, half, every, right)
+        store(high_qkv.at[1, part], g_qkv.at[1, part])
+        store(high_qkv.at[2, part], g_qkv.at[2, part])
+    for i in range(2):
+        for part, name, start in ((first, "0", 0), (second, "1", half)):
+            loads["back" + str(i) + name].wait()
+            cast(high_back.at[i], low_back.at[i], start, half, every, every)
+            store(high_back.at[i, part], g_back.at[i, part])
+            loads["in" + str(i) + name].wait()
+            cast(high_in.at[i], low_in.at[i], start, half, every, every)
+            lanes = pl.ds(i * wide, wide)
+            store(high_in.at[i, part], g_inner.at[part, lanes])
     for item in stores:
         item.wait()
-
-
-def widen(back_a, back_b, inner_a, inner_b, query, out_low, out_high, pair, vec, out_in, grad_in, *outs):
-    out, in_grad, g_back, g_inner, g_qkv, g_out, g_qv, g_in_bias, *vectors = outs
-    col = query.shape[1]
-    wide = vectors[0].shape[0]
-    out[...] = out_in[...]
-    in_grad[...] = grad_in[...]
-    g_back[0] = back_a[...].astype(F32)
-    g_back[1] = back_b[...].astype(F32)
-    half = inner_a.shape[1]
-    g_inner[:, :half] = inner_a[...].astype(F32)
-    g_inner[:, half:] = inner_b[...].astype(F32)
-    g_qkv[0] = query[...].astype(F32)
-    g_qkv[1] = pair[:, :col].astype(F32)
-    g_qkv[2] = pair[:, col:].astype(F32)
-    g_out[:, :col] = out_low[...].astype(F32)
-    g_out[:, col:] = out_high[...].astype(F32)
-
-    @pl.when(pl.program_id(0) == 0)
-    def _():
-        full = vec[...].astype(F32)
-
-        def line(row, count):
-            return jnp.concatenate([full[r : r + 1, :] for r in range(row, row + count)], 1)
-
-        per = wide // 128
-        for i, vector in enumerate(vectors):
-            vector[...] = line(i * per, per).reshape(wide)
-        row = len(vectors) * per
-        g_qv[...] = jnp.concatenate(
-            [line(row, col // 128), line(row + col // 128, col // 128)], 0
-        )
-        g_in_bias[...] = line(row + 2 * col // 128, g_in_bias.shape[0] // 128).reshape(
-            g_in_bias.shape[0]
-        )
 
 
 def body(
@@ -907,7 +993,6 @@
         vmem((2, tok, wide), BF16),
         vmem((2, tok, wide), BF16),
         vmem((2, tok, wide), BF16),
-        vmem((2, tok, wide), BF16),
         vmem((3, wide, col), BF16),
         vmem((col, wide), BF16),
         vmem((wide, ff), BF16),
@@ -929,7 +1014,7 @@
         vmem((2, tok, 128), F32),
         vmem((2 * tok, wide), BF16),
         vmem((2 * tok, ff), BF16),
-        vmem((2, tok, ff), F32),
+        vmem((2, tok, ff), BF16),
         vmem((2, tok, wide), F32),
         vmem((2 * tok, wide), BF16),
         vmem((2 * tok, ff), BF16),
@@ -950,6 +1035,7 @@
     scratch += [vmem((r - r // 16, w), BF16) for r, w in parts]
     if upper:
         scratch += [vmem((upper, r // 16, w), BF16) for r, w in parts]
+    scratch += [vmem(shape, BF16) for shape in parts]
     scratch += [
         pltpu.SemaphoreType.DMA((COPIES,)),
         pltpu.SemaphoreType.DMA((COPIES,)),
@@ -969,7 +1055,7 @@
         out_specs=[any_spec] * 9,
         scratch_shapes=scratch,
         compiler_params=pltpu.CompilerParams(
-            collective_id=0, has_side_effects=True, vmem_limit_bytes=63 * 1024 * 1024
+            collective_id=0, has_side_effects=True, vmem_limit_bytes=65_000 * 1024
         ),
         cost_estimate=pl.CostEstimate(
             flops=12_000_000_000, bytes_accessed=40_000_000, transcendentals=8_000_000
@@ -995,13 +1081,9 @@
         short_random,
         long_random,
     )
-    steps = 8
     vector = jax.ShapeDtypeStruct((wide,), F32)
-    whole = pl.BlockSpec(memory_space=pltpu.VMEM)
-    rows_spec = pl.BlockSpec((2, tok // steps, wide), lambda i: (0, i, 0))
     out, in_grad, g_back, g_inner, g_qkv, g_out, g_qv, g_in_bias, *vectors = pl.pallas_call(
         widen,
-        grid=(steps,),
         out_shape=[
             jax.ShapeDtypeStruct(inputs.shape, BF16),
             jax.ShapeDtypeStruct(inputs.shape, BF16),
@@ -1013,31 +1095,27 @@
             jax.ShapeDtypeStruct((ff,), F32),
         ]
         + [vector] * 6,
-        in_specs=[
-            pl.BlockSpec((ff // 2 // steps, wide), lambda i: (i, 0)),
-            pl.BlockSpec((ff // 2 // steps, wide), lambda i: (i, 0)),
-            pl.BlockSpec((wide // steps, ff // 2), lambda i: (i, 0)),
-            pl.BlockSpec((wide // steps, ff // 2), lambda i: (i, 0)),
-            pl.BlockSpec((wide // steps, col), lambda i: (i, 1)),
-            pl.BlockSpec((col // steps, col), lambda i: (i, 0)),
-            pl.BlockSpec((col // steps, col), lambda i: (i + steps, 0)),
-            pl.BlockSpec((wide // steps, 2 * col), lambda i: (i, 0)),
-            whole,
-            rows_spec,
-            rows_spec,
+        in_specs=[any_spec] * 9,
+        out_specs=[any_spec] * 6 + [vmem_spec] * 8,
+        scratch_shapes=[
+            vmem((2, wide, wide), BF16),
+            vmem((2, wide, wide), BF16),
+            vmem((wide, 2 * col), BF16),
+            vmem((wide, 2 * col), BF16),
+            vmem((VEC_ROWS, 128), BF16),
+            vmem((2, wide, wide), F32),
+            vmem((2, wide, wide), F32),
+            vmem((3, wide, col), F32),
+            vmem((col, wide), F32),
+            pltpu.SemaphoreType.DMA((16,)),
+            pltpu.SemaphoreType.DMA((20,)),
+            pltpu.SemaphoreType.DMA((2,)),
+            vmem(inputs.shape, BF16),
+            vmem(inputs.shape, BF16),
         ],
-        out_specs=[
-            rows_spec,
-            rows_spec,
-            pl.BlockSpec((2, ff // 2 // steps, wide), lambda i: (0, i, 0)),
-            pl.BlockSpec((wide // steps, ff), lambda i: (i, 0)),
-            pl.BlockSpec((3, wide // steps, col), lambda i: (0, i, 0)),
-            pl.BlockSpec((col // steps, wide), lambda i: (i, 0)),
-        ]
-        + [whole] * 8,
         compiler_params=pltpu.CompilerParams(vmem_limit_bytes=63 * 1024 * 1024),
         name="widen",
-    )(s_back_a, s_back_b, s_in_a, s_in_b, s_query, s_query, s_query, s_pair, s_vec, out, in_grad)
+    )(s_back_a, s_back_b, s_in_a, s_in_b, s_query, s_pair, s_vec, out, in_grad)
     return (
         out,
         in_grad,

time: 171 us -> 168 us (0.982)
  Pallas kernels: 169 us -> 167 us
    pallas_call x1, Pallas kernels: 159 us -> 157 us  [body(): pl.pallas_call(functools.partial(kernel, seq_count), out_shape=[jax.Shape...]
where the time goes in v4:
time: 168 us
  Pallas kernels  167 us (99%)
    pallas_call x1, Pallas kernels, body(): pl.pallas_call(functools.partial(kernel, seq_count), out_shape=[jax.Shape...  157 us
    pallas_call x1, Pallas kernels, body(): pl.pallas_call(widen, out_shape=[jax.ShapeDtypeStruct(inputs.shape, BF16)...  9.73 us

profile of v4, /device:TPU:0, one launch (start us, length us, event | category | flops | bytes accessed | tf_op | source)
XLA Modules:
  0.0 167.6 jit_solution(6986878240289086822)
XLA Ops:
  0.7 157.0 %layer.1 = (bf16[2,256,768]{2,1,0:T(8,128)(2,1)}, bf16[2,256,768]{2,1,0:T(8,128)(2,1)}, bf16[768,768]{1,0:T(8,128)(2,1)}, bf16[768,768]{1,0:T(8,128)(2,1)}, bf16...) custom-call(bf16[2,256,768]{2,1,0:T(8,128)(2,1)} %x_in.1, ...), custom_call_target="tpu_custom_call" | custom-call | flops 12000000000 | bytes 40000000 | tf_op jit(solution)/shard_map/layer/pallas_call | solution.py:1047
  157.7 9.7 %widen.1 = (bf16[2,256,768]{2,1,0:T(8,128)(2,1)}, bf16[2,256,768]{2,1,0:T(8,128)(2,1)}, f32[2,768,768]{2,1,0:T(8,128)}, f32[768,1536]{1,0:T(8,128)}, f32[3,768,3...) custom-call(bf16[768,768]{1,0:T(8,128)(2,1)} %get-tuple-element.37.s, ...), custom_call_target="tpu_custom_call" | custom-call | tf_op jit(solution)/shard_map/widen/pallas_call | solution.py:1085

commit v5 on v4

--- a/solution.py
+++ b/solution.py
@@ -530,13 +530,16 @@
     posts[0, LONG].wait_send()
     posts[1, SHORT] = post(1, SHORT)
     feed_forward(LONG)
+    posts[1, SHORT].wait_send()
     posts[1, LONG] = post(1, LONG)
 
     def norm_back(grad, normed, root):
         return root * (grad - mean(grad) - normed * mean(grad * normed))
 
     def feed_norm(mb):
-        posts[1, mb].wait()
+        posts[1, mb].wait_recv()
+        if mb == LONG:
+            posts[1, mb].wait_send()
 
         def norm_step(r):
             rows = aligned(r * tile_rows, tile_rows, tile_rows)

time: 168 us -> 167 us (level)
  no operation moved by 1% of the time
where the time goes in v5:
time: 167 us
  Pallas kernels  166 us (99%)
    pallas_call x1, Pallas kernels, body(): pl.pallas_call(functools.partial(kernel, seq_count), out_shape=[jax.Shape...  156 us
    pallas_call x1, Pallas kernels, body(): pl.pallas_call(widen, out_shape=[jax.ShapeDtypeStruct(inputs.shape, BF16)...  9.73 us

profile of v5, /device:TPU:0, one launch (start us, length us, event | category | flops | bytes accessed | tf_op | source)
XLA Modules:
  0.0 167.0 jit_solution(18412491324396136917)
XLA Ops:
  0.7 156.5 %layer.1 = (bf16[2,256,768]{2,1,0:T(8,128)(2,1)}, bf16[2,256,768]{2,1,0:T(8,128)(2,1)}, bf16[768,768]{1,0:T(8,128)(2,1)}, bf16[768,768]{1,0:T(8,128)(2,1)}, bf16...) custom-call(bf16[2,256,768]{2,1,0:T(8,128)(2,1)} %x_in.1, ...), custom_call_target="tpu_custom_call" | custom-call | flops 12000000000 | bytes 40000000 | tf_op jit(solution)/shard_map/layer/pallas_call | solution.py:1050
  157.2 9.7 %widen.1 = (bf16[2,256,768]{2,1,0:T(8,128)(2,1)}, bf16[2,256,768]{2,1,0:T(8,128)(2,1)}, f32[2,768,768]{2,1,0:T(8,128)}, f32[768,1536]{1,0:T(8,128)}, f32[3,768,3...) custom-call(bf16[768,768]{1,0:T(8,128)(2,1)} %get-tuple-element.37.s, ...), custom_call_target="tpu_custom_call" | custom-call | tf_op jit(solution)/shard_map/widen/pallas_call | solution.py:1088
